TPU v7x, 128 devices: a whole 4x4x4 slice. The times are simulated.
128 devices in a mesh: rep: 8 (over z_hi, x), fsdp: 16 (over z_lo, y, core).
Axes of the slice: x: 4, y: 4, z: 4 (z_hi: 2, z_lo: 2; z = z_hi * 2 + z_lo), core: 2. Of those that a mesh axis runs over, the one named last changes fastest.
Arguments:
- round_index: int32 [], replicated, may hold values from 0 to 999
- tokens: bfloat16 [8, 8192, 8192], P('rep', 'fsdp'), may hold values from -6 to 6
- cotangent: bfloat16 [8, 8192, 1024], P('rep', 'fsdp'), may hold values from -6 to 6
- params: float32 [8, 8192, 1024], P('rep', 'fsdp'), may hold values from -6 to 6
- momentum: float32 [8, 8192, 1024], P('rep', 'fsdp'), may hold values from -6 to 6
Outputs:
- key_out: bfloat16 [8, 8192, 1024], P('rep', 'fsdp')
- input_grad: bfloat16 [8, 8192, 8192], P('rep', 'fsdp')
- new_params: float32 [8, 8192, 1024], P('rep', 'fsdp')
- new_momentum: float32 [8, 8192, 1024], P('rep', 'fsdp')
All inputs are finite; a program needn't handle non-finite values.
Results may differ from a plain program's by a relative error of at most 0.018.
Values may be sent and summed in bfloat16 or wider, within the bound.
No kernel may reach another device: no remote copies, remote signals or barrier semaphores. Data moves between devices by JAX's collectives and lax.ppermute only.
A program may use at most 256 MiB of HBM per device.

v0:
```python
import jax
import jax.numpy as jnp
from jax import lax
from jax.experimental import pallas as pl
from jax.experimental.pallas import tpu as pltpu
from jax.sharding import PartitionSpec as P

D = 8192
KV = 1024
ROWS = 512
NZ, NY, NC = 2, 4, 2
SCALE = D ** (-0.5)
LEVELS = 3
TN = (((0,), (0,)), ((), ()))
NT = (((1,), (1,)), ((), ()))
NN = (((1,), (0,)), ((), ()))
F32, BF16 = jnp.float32, jnp.bfloat16

FAR = ((1, 2),)
MIDDLE = ((1, 1), (1, -1), (0, 2))
NEAR = ((0, -1), (0, 1), (1, 0), (0, 0))


def place(z, y, c):
    return (z % NZ) * NY * NC + (y % NY) * NC + c % NC


def shift(dz=0, dy=0, dc=0):
    return [
        (place(z, y, c), place(z + dz, y + dy, c + dc))
        for z in range(NZ)
        for y in range(NY)
        for c in range(NC)
    ]


def y_up(value):
    return lax.ppermute(value, "fsdp", shift(dy=1))


def y_down(value):
    return lax.ppermute(value, "fsdp", shift(dy=-1))


def z_across(value):
    return lax.ppermute(value, "fsdp", shift(dz=1))


def core_swap(value):
    return lax.ppermute(value, "fsdp", shift(dc=1))


def partner_swap(value, bit):
    def swap(arr, level):
        return lax.ppermute(arr, "rep", [(r, r ^ (1 << level)) for r in range(1 << LEVELS)])

    return lax.switch(bit, [lambda arr, level=level: swap(arr, level) for level in range(LEVELS)], value)


def columns(offsets, core):
    f = lax.axis_index("fsdp").astype(jnp.int32)
    z, y = f // (NY * NC), (f // NC) % NY
    return jnp.stack([place(z + dz, y + dy, core).astype(jnp.int32) for dz, dy in offsets])


def dot(a, b, dims):
    return lax.dot_general(a, b, dims, preferred_element_type=F32)


def whole(shape):
    return pl.BlockSpec(shape, lambda k, idx: (0,) * len(shape))


def by_column():
    return pl.BlockSpec((ROWS, ROWS), lambda k, idx: (0, idx[k]))


def by_step(start=0):
    return pl.BlockSpec((1, ROWS, ROWS), lambda k, idx: (k + start, 0, 0))


def params_of(flops, nbytes, vmem=36):
    flops, nbytes = int(flops), int(nbytes)
    return dict(
        compiler_params=pltpu.CompilerParams(vmem_limit_bytes=vmem * 2**20),
        cost_estimate=pl.CostEstimate(flops=flops, bytes_accessed=nbytes, transcendentals=0),
    )


ANYWHERE = pl.BlockSpec(memory_space=pl.ANY)
IN_HBM = pl.BlockSpec(memory_space=pltpu.HBM)


def slab(idx_ref, k):
    return pl.ds(pl.multiple_of(idx_ref[k] * ROWS, ROWS), ROWS)


def token_slabs(idx_ref, tok_ref, buf, sem, n):
    step = pl.program_id(0)

    def copy(k):
        return pltpu.make_async_copy(tok_ref.at[:, slab(idx_ref, k)], buf.at[k], sem.at[k])

    @pl.when(step == 0)
    def _():
        for k in range(n):
            copy(k).start()

    for k in range(n):

        @pl.when(step == k)
        def _(k=k):
            copy(k).wait()

    return buf[step]


def slab_scratch(n):
    return [pltpu.VMEM((n, ROWS, ROWS), BF16), pltpu.SemaphoreType.DMA((n,))]


def through(in_copies, out_copies):
    for copy in in_copies:
        copy.start()
    for copy, out in zip(in_copies, out_copies):
        copy.wait()
        out.start()
    for out in out_copies:
        out.wait()


def pack_first(tokens, cot, idx, after):
    def kernel(idx_ref, tok_ref, cot_ref, after_ref, out_ref, buf, sem, out_sem):
        del after_ref
        n, rows = 4, ROWS // 4
        ins, outs = [], []
        for i in range(n):
            part = pl.ds(i * rows, rows)
            tok_part, tok_buf = tok_ref.at[part, slab(idx_ref, 0)], buf.at[part, pl.ds(KV, ROWS)]
            ins.append(pltpu.make_async_copy(cot_ref.at[part], buf.at[part, pl.ds(0, KV)], sem.at[i]))
            ins.append(pltpu.make_async_copy(tok_part, tok_buf, sem.at[n + i]))
            outs.append(pltpu.make_async_copy(buf.at[part], out_ref.at[part], out_sem.at[i]))
        for copy in ins:
            copy.start()
        for i in range(n):
            ins[2 * i].wait()
            ins[2 * i + 1].wait()
            outs[i].start()
        for copy in outs:
            copy.wait()

    shape = (ROWS, KV + ROWS)
    return pl.pallas_call(
        kernel,
        grid_spec=pltpu.PrefetchScalarGridSpec(
            num_scalar_prefetch=1,
            grid=(1,),
            in_specs=[IN_HBM, ANYWHERE, ANYWHERE],
            out_specs=ANYWHERE,
            scratch_shapes=[
                pltpu.VMEM(shape, BF16),
                pltpu.SemaphoreType.DMA((8,)),
                pltpu.SemaphoreType.DMA((4,)),
            ],
        ),
        out_shape=jax.ShapeDtypeStruct(shape, BF16),
        name="pack_first",
        **params_of(0, 3 * 2**20, 58),
    )(idx, tokens, cot, after)


def pack(tokens, idx, after):
    n = idx.shape[0]

    def kernel(idx_ref, tok_ref, after_ref, out_ref, buf, sem, out_sem):
        del after_ref
        through(
            [
                pltpu.make_async_copy(tok_ref.at[:, slab(idx_ref, k)], buf.at[k], sem.at[k])
                for k in range(n)
            ],
            [pltpu.make_async_copy(buf.at[k], out_ref.at[k], out_sem.at[k]) for k in range(n)],
        )

    return pl.pallas_call(
        kernel,
        grid_spec=pltpu.PrefetchScalarGridSpec(
            num_scalar_prefetch=1,
            grid=(1,),
            in_specs=[IN_HBM, ANYWHERE],
            out_specs=ANYWHERE,
            scratch_shapes=[
                pltpu.VMEM((n, ROWS, ROWS), BF16),
                pltpu.SemaphoreType.DMA((n,)),
                pltpu.SemaphoreType.DMA((n,)),
            ],
        ),
        out_shape=jax.ShapeDtypeStruct((n, ROWS, ROWS), BF16),
        name="pack",
        **params_of(0, n * 2**20, 58),
    )(idx, tokens, after)


def unpack(target, pieces, idx):
    n = idx.shape[0]

    def kernel(idx_ref, old_ref, piece_ref, out_ref, buf, sem, out_sem):
        del old_ref
        through(
            [pltpu.make_async_copy(piece_ref.at[k], buf.at[k], sem.at[k]) for k in range(n)],
            [
                pltpu.make_async_copy(buf.at[k], out_ref.at[:, slab(idx_ref, k)], out_sem.at[k])
                for k in range(n)
            ],
        )

    return pl.pallas_call(
        kernel,
        grid_spec=pltpu.PrefetchScalarGridSpec(
            num_scalar_prefetch=1,
            grid=(1,),
            in_specs=[ANYWHERE] * 2,
            out_specs=ANYWHERE,
            scratch_shapes=[
                pltpu.VMEM((n, ROWS, ROWS), BF16),
                pltpu.SemaphoreType.DMA((n,)),
                pltpu.SemaphoreType.DMA((n,)),
            ],
        ),
        out_shape=jax.ShapeDtypeStruct(target.shape, BF16),
        input_output_aliases={1: 0},
        name="unpack",
        **params_of(0, n * 2**20),
    )(idx, target, pieces)


def cut_rows(parts):
    n = len(parts)

    def kernel(*refs):
        ins, outs, (buf, sem, out_sem) = refs[:n], refs[n : 2 * n], refs[2 * n :]
        spans = [pl.ds(lo, hi - lo) for _, lo, hi in parts]
        through(
            [
                pltpu.make_async_copy(r.at[d], buf.at[d], sem.at[i])
                for i, (r, d) in enumerate(zip(ins, spans))
            ],
            [
                pltpu.make_async_copy(buf.at[d], r, out_sem.at[i])
                for i, (r, d) in enumerate(zip(outs, spans))
            ],
        )

    return pl.pallas_call(
        kernel,
        in_specs=[ANYWHERE] * n,
        out_specs=[ANYWHERE] * n,
        out_shape=[jax.ShapeDtypeStruct((hi - lo, KV), BF16) for _, lo, hi in parts],
        scratch_shapes=[
            pltpu.VMEM((ROWS, KV), BF16),
            pltpu.SemaphoreType.DMA((n,)),
            pltpu.SemaphoreType.DMA((n,)),
        ],
        name="cut_rows",
        **params_of(0, 2 * 2**20),
    )(*[array for array, _, _ in parts])


def join_rows(pieces, bounds, after):
    n, m = len(pieces), len(after)

    def kernel(*refs):
        ins, out, (buf, sem, out_sem) = refs[:n], refs[n + m], refs[n + m + 1 :]
        spans = [pl.ds(lo, hi - lo) for lo, hi in bounds]
        through(
            [
                pltpu.make_async_copy(r, buf.at[d], sem.at[i])
                for i, (r, d) in enumerate(zip(ins, spans))
            ],
            [
                pltpu.make_async_copy(buf.at[d], out.at[d], out_sem.at[i])
                for i, d in enumerate(spans)
            ],
        )

    return pl.pallas_call(
        kernel,
        in_specs=[ANYWHERE] * (n + m),
        out_specs=ANYWHERE,
        out_shape=jax.ShapeDtypeStruct((ROWS, KV), BF16),
        scratch_shapes=[
            pltpu.VMEM((ROWS, KV), BF16),
            pltpu.SemaphoreType.DMA((n,)),
            pltpu.SemaphoreType.DMA((n,)),
        ],
        name="join_rows",
        **params_of(0, 2 * 2**20),
    )(*pieces, *after)


def held_until(values, after):
    n, m = len(values), len(after)

    def kernel(*refs):
        del refs

    return pl.pallas_call(
        kernel,
        in_specs=[ANYWHERE] * (n + m),
        out_specs=[ANYWHERE] * n,
        out_shape=[jax.ShapeDtypeStruct(v.shape, v.dtype) for v in values],
        input_output_aliases={i: i for i in range(n)},
        name="held_until",
        **params_of(0, 0),
    )(*values, *after)


def gradients(tokens, other_tokens, cot, first, idx, start=0, cuts=None, after=()):
    n = idx.shape[0]
    if cuts is None:
        shapes = [(ROWS, KV)] * n
    else:
        shapes = [(hi - lo, KV) for lo, hi in cuts]

    def kernel(idx_ref, tok_ref, oth_ref, cot_ref, cot_oth_ref, *outs):
        *outs, tok_buf, tok_sem = outs[len(after) :]
        tok = token_slabs(idx_ref, tok_ref, tok_buf, tok_sem, n)
        step = pl.program_id(0)
        oth = oth_ref[...] if cuts is not None else oth_ref[0]
        total = dot(tok, cot_ref[...], TN) + dot(oth, cot_oth_ref[...], TN)
        total = (total * SCALE).astype(BF16)
        if cuts is not None:
            for (lo, hi), out in zip(cuts, outs):
                out[...] = total[lo:hi]
        else:
            for i, out in enumerate(outs):

                @pl.when(step == i)
                def _(out=out):
                    out[...] = total

    if cuts is not None:
        oth_spec = pl.BlockSpec((ROWS, ROWS), lambda k, idx: (0, KV // ROWS))
    else:
        oth_spec = by_step(start)
    return pl.pallas_call(
        kernel,
        grid_spec=pltpu.PrefetchScalarGridSpec(
            num_scalar_prefetch=1,
            grid=(n,),
            in_specs=[IN_HBM, oth_spec, whole((ROWS, KV)), whole((ROWS, KV))]
            + [ANYWHERE] * len(after),
            out_specs=[whole(s) for s in shapes],
            scratch_shapes=slab_scratch(n),
        ),
        out_shape=[jax.ShapeDtypeStruct(s, BF16) for s in shapes],
        name="gradients",
        **params_of(n * 4 * ROWS * ROWS * KV, (2 * n + 2) * 2**20, 58 if n == 1 else 36),
    )(idx, tokens, other_tokens, cot, first, *after)


def forward(tokens, other_tokens, cot, first, weights, idx, start, after, keys=None, grad_in=None):
    n, m = idx.shape[0], len(after)
    last = keys is not None

    def kernel(idx_ref, tok_ref, oth_ref, cot_ref, cot_oth_ref, *refs):
        w_refs, rest = refs[:n], refs[n + m :]
        if last:
            own_in, oth_in, _, own_out, oth_out, gi_ref, back_ref, *rest, acc = rest
        else:
            own_out, oth_out, gi_ref, back_ref, *rest = rest
            acc = oth_out
        w_buf, sem, tok_buf, tok_sem = rest
        step = pl.program_id(0)

        @pl.when(step == 0)
        def _():
            for i, w_ref in enumerate(w_refs):
                pltpu.make_async_copy(w_ref, w_buf.at[i], sem.at[i]).start()
            if last:
                own_out[...] = own_in[...]
                acc[...] = oth_in[...]
            else:
                own_out[...] = jnp.zeros_like(own_out)
                acc[...] = jnp.zeros_like(acc)

        for i, w_ref in enumerate(w_refs):

            @pl.when(step == i)
            def _(i=i, w_ref=w_ref):
                pltpu.make_async_copy(w_ref, w_buf.at[i], sem.at[i]).wait()

        w = w_buf[step]
        tok = token_slabs(idx_ref, tok_ref, tok_buf, tok_sem, n)
        own_out[...] += dot(tok, w, NN)
        acc[...] += dot(oth_ref[0], w, NN)
        gi_ref[...] = (dot(cot_ref[...], w, NT) * SCALE).astype(BF16)
        back_ref[0] = (dot(cot_oth_ref[...], w, NT) * SCALE).astype(BF16)

        if last:

            @pl.when(step == n - 1)
            def _():
                oth_out[...] = (acc[...] * SCALE).astype(BF16)

    in_specs = [IN_HBM, by_step(start), whole((ROWS, KV)), whole((ROWS, KV))]
    in_specs += [ANYWHERE] * (n + m)
    operands = [tokens, other_tokens, cot, first, *weights, *after]
    aliases = {}
    scratch = [pltpu.VMEM((n, ROWS, KV), BF16), pltpu.SemaphoreType.DMA((n,)), *slab_scratch(n)]
    if last:
        in_specs += [whole((ROWS, KV))] * 2 + [ANYWHERE]
        operands += [*keys, grad_in]
        aliases = {len(operands): 2}
        scratch += [pltpu.VMEM((ROWS, KV), F32)]
    return pl.pallas_call(
        kernel,
        grid_spec=pltpu.PrefetchScalarGridSpec(
            num_scalar_prefetch=1,
            grid=(n,),
            in_specs=in_specs,
            out_specs=[whole((ROWS, KV)), whole((ROWS, KV)), by_column(), by_step()],
            scratch_shapes=scratch,
        ),
        out_shape=[
            jax.ShapeDtypeStruct((ROWS, KV), F32),
            jax.ShapeDtypeStruct((ROWS, KV), BF16 if last else F32),
            jax.ShapeDtypeStruct((ROWS, D), BF16),
            jax.ShapeDtypeStruct((n, ROWS, ROWS), BF16),
        ],
        input_output_aliases=aliases,
        name="forward",
        **params_of(n * 8 * ROWS * ROWS * KV, (3 * n + 8) * 2**20),
    )(idx, *operands)


def one_shard(tokens, cot, weights, keys, grad_in, idx, received=None):
    final = received is not None
    tile = ROWS // 2

    def kernel(idx_ref, tok_ref, cot_ref, w_ref, key_ref, *rest):
        *rest, tok_buf, sem = rest
        step, n = pl.program_id(0), ROWS // tile
        part = [pl.ds(i * tile, tile) for i in range(n)]
        copies = [
            pltpu.make_async_copy(tok_ref.at[p, slab(idx_ref, 0)], tok_buf.at[p], sem.at[i])
            for i, p in enumerate(part)
        ]

        @pl.when(step == 0)
        def _():
            for copy in copies:
                copy.start()

        for i, copy in enumerate(copies):

            @pl.when(step == i)
            def _(copy=copy):
                copy.wait()

        tok = tok_buf[pl.ds(pl.multiple_of(step * tile, tile), tile)]
        total = key_ref[...] + dot(tok, w_ref[...], NN)
        if final:
            rec_ref, _, key_out, gi_ref = rest
            key_out[...] = (total * SCALE + rec_ref[...].astype(F32)).astype(BF16)
        else:
            _, key_out, gi_ref = rest
            key_out[...] = total
        gi_ref[...] = (dot(cot_ref[...], w_ref[...], NT) * SCALE).astype(BF16)

    def wide():
        return pl.BlockSpec((tile, KV), lambda k, idx: (k, 0))

    def narrow():
        return pl.BlockSpec((tile, ROWS), lambda k, idx: (k, idx[0]))

    operands = [tokens, cot, weights, keys] + ([received] if final else []) + [grad_in]
    return pl.pallas_call(
        kernel,
        grid_spec=pltpu.PrefetchScalarGridSpec(
            num_scalar_prefetch=1,
            grid=(ROWS // tile,),
            in_specs=[IN_HBM, wide(), whole((ROWS, KV)), wide()]
            + ([wide()] if final else [])
            + [ANYWHERE],
            out_specs=[wide(), narrow()],
            scratch_shapes=[
                pltpu.VMEM((ROWS, ROWS), BF16),
                pltpu.SemaphoreType.DMA((ROWS // tile,)),
            ],
        ),
        out_shape=[
            jax.ShapeDtypeStruct((ROWS, KV), BF16 if final else F32),
            jax.ShapeDtypeStruct((ROWS, D), BF16),
        ],
        input_output_aliases={len(operands): 1},
        name="one_shard",
        **params_of(4 * ROWS * ROWS * KV, 8 * 2**20),
    )(idx, *operands)


def body(round_index, tokens, cotangent, params, momentum):
    tokens, cot, params, momentum = tokens[0], cotangent[0], params[0], momentum[0]
    bit = jnp.mod(round_index, LEVELS)
    half, cut, end = ROWS // 2, 176, 336
    core = lax.axis_index("fsdp").astype(jnp.int32) % NC
    far, far_oth = columns(FAR, core), columns(FAR, 1 - core)
    mid, mid_oth = columns(MIDDLE, core), columns(MIDDLE, 1 - core)
    near, near_oth = columns(NEAR, core), columns(NEAR, 1 - core)
    rest, rest_oth = columns(MIDDLE + NEAR, core), columns(MIDDLE + NEAR, 1 - core)

    own = params.astype(BF16)
    w_0m, w_01, w_10 = y_up(own), y_down(own), z_across(own)

    packed = pack_first(tokens, cot, far_oth, own)
    first = core_swap(packed)
    others = core_swap(pack(tokens, rest_oth, packed))

    t0, t1 = gradients(tokens, first, cot, first, far, cuts=((0, half), (half, ROWS)))
    (t1,) = held_until((t1,), (others,))
    t0, t1 = y_up(t0), y_down(t1)
    p_11, p_1m, p_02, p_0m, p_01, p_10, p_00 = gradients(
        tokens, others, cot, first, rest
    )
    p_11 = p_11.at[:half].add(t0)
    p_1m = p_1m.at[half:].add(t1)
    p_11, p_1m, p_02 = held_until((p_11, p_1m, p_02), (w_0m, w_01, w_10))
    key_own, key_oth, grad_in, back = forward(
        tokens, others, cot, first, (w_0m, w_01, w_10, own), near, len(MIDDLE), (p_11, p_1m, p_02)
    )
    p_11, p_1m, p_02 = y_up(p_11), z_across(p_1m), y_down(p_02)
    p_0m = (p_0m.astype(F32) + p_1m.astype(F32) + p_02.astype(F32)).astype(BF16)
    p_10 = (p_10.astype(F32) + p_11.astype(F32)).astype(BF16)
    p_01, own = held_until((p_01, own), (key_own, p_0m, p_10))
    p_0m, p_01, p_10 = y_down(p_0m), y_up(p_01), z_across(p_10)
    partner_params = partner_swap(own, bit)
    gradient = (p_00.astype(F32) + p_01.astype(F32)) + (p_0m.astype(F32) + p_10.astype(F32))
    moved = 0.9 * momentum + gradient

    grad_in = unpack(grad_in, core_swap(back), near_oth)
    w_0m, w_10 = held_until((w_0m, w_10), (p_0m, p_01, p_10, partner_params))
    w_02, w_11, w_1m = y_up(w_0m), y_down(w_10), z_across(w_0m)
    partner_moved = partner_swap(moved.astype(BF16), bit)
    bounds = (0, cut), (cut, end), (end, ROWS)
    pieces = [w[lo:hi] for w, (lo, hi) in zip((w_1m, w_11, w_02), bounds)]
    thirds = y_up(pieces[0]), y_down(pieces[1]), z_across(pieces[2])
    theirs = partner_moved.astype(F32)
    new_momentum = 0.5 * (moved + theirs)
    partner_stepped = partner_params.astype(F32) - 0.1 * theirs
    new_params = 0.5 * ((params - 0.1 * moved) + partner_stepped)
    key_own, key_oth, grad_in, back = forward(
        tokens,
        others,
        cot,
        first,
        (w_11, w_1m, w_02),
        mid,
        0,
        (partner_moved, *pieces),
        (key_own, key_oth),
        grad_in,
    )
    key_oth = core_swap(key_oth)
    (w_12,) = held_until((jnp.concatenate(thirds, axis=0),), (new_params, new_momentum))
    w_12_oth = core_swap(w_12)
    grad_in = unpack(grad_in, core_swap(back), mid_oth)
    key_own, grad_in = one_shard(tokens, cot, w_12, key_own, grad_in, far)
    key_out, grad_in = one_shard(tokens, cot, w_12_oth, key_own, grad_in, far_oth, key_oth)
    return key_out[None], grad_in[None], new_params[None], new_momentum[None]


def solution(mesh):
    rows = P("rep", "fsdp", None)
    return jax.shard_map(
        body,
        mesh=mesh,
        in_specs=(P(), rows, rows, rows, rows),
        out_specs=(rows, rows, rows, rows),
        check_vma=False,
    )
```

profile of v0, /device:TPU:1, one launch (start us, length us, event | category | flops | bytes accessed | tf_op | source)
XLA Modules:
  0.0 178.5 jit_solution(9993219187425238250)
XLA Ops:
  0.8 2.7 %bitcast_convert_fusion.after_ref.refs_3_.refs_1_ = bf16[512,1024]{1,0:T(8,128)(2,1)} fusion(f32[1,512,1024]{2,1,0:T(8,128)} %param.18), kind=kLoop, calls=%fused_computation.8 | loop fusion | flops 524288 | bytes 3145728 | tf_op jit(solution)/shard_map/convert_element_type | solution.py:512
  3.5 2.2 %pack_first.1.after_ref = bf16[512,1536]{1,0:T(8,128)(2,1)} custom-call(s32[1]{0:T(128)} %bitcast.idx_ref, bf16[512,8192]{1,0:T(8,128)(2,1)} %bitcast.30, bf16[512,1024]{1,0:T(8,128)(2,1)} %bitcast.40, bf16[512,1024]{1,0:T(8,128)(2,1)} %bitcast_convert_fusion.after_ref.refs_3_.refs_1_), custom_call_target="tpu_custom_call" | custom-call | bytes 3145728 | tf_op jit(solution)/shard_map/pack_first/pallas_call | solution.py:153
  6.4 3.8 %pack.1 = bf16[7,512,512]{2,1,0:T(8,128)(2,1)} custom-call(s32[7]{0:T(128)} %stack.96.idx_ref, bf16[512,8192]{1,0:T(8,128)(2,1)} %bitcast.31, bf16[512,1536]{1,0:T(8,128)(2,1)} %pack_first.1.after_ref), custom_call_target="tpu_custom_call" | custom-call | bytes 7340032 | tf_op jit(solution)/shard_map/pack/pallas_call | solution.py:185
  10.2 1.5 collective-permute-start.8
  11.8 1.4 collective-permute-start.6
  13.2 1.6 collective-permute-start.7
  14.8 1.4 collective-permute-start.12
  16.3 3.7 %collective-permute-done.9.cot_oth_ref.oth_ref = bf16[512,1536]{1,0:T(8,128)(2,1)S(1)} collective-permute-done((bf16[512,1536]{1,0:T(8,128)(2,1)}, bf16[512,1536]{1,0:T(8,128)(2,1)S(1)}, u32[]{:S(2)}, u32[]{:S(2)}) %collective-permute-start.9) | collective-permute-done | bytes 1572896 | tf_op jit(solution)/shard_map/ppermute | solution.py:50
  20.0 1.1 copy-done.1
  21.2 4.9 %gradients.3 = (bf16[256,1024]{1,0:T(8,128)(2,1)}, bf16[256,1024]{1,0:T(8,128)(2,1)}) custom-call(s32[1]{0:T(128)} %bitcast.18.idx_ref, bf16[512,8192]{1,0:T(8,128)(2,1)} %bitcast.32, bf16[512,1536]{1,0:T(8,128)(2,1)} %copy-done.1, bf16[512,1024]{1,0:T(8,128)(2,1)} %bitcast.41, bf16[512,1536]{1,0:T(8,128)(2,1)} %copy-done.1), custom_call_target="tpu_custom_call" | custom-call | flops 1073741824 | bytes 4194304 | tf_op jit(solution)/shard_map/gradients/pallas_call | solution.py:346
  26.1 1.4 collective-permute-start.10
  27.6 1.5 collective-permute-start.11
  29.3 14.2 %gradients.2 = (bf16[512,1024]{1,0:T(8,128)(2,1)S(1)}, bf16[512,1024]{1,0:T(8,128)(2,1)S(1)}, bf16[512,1024]{1,0:T(8,128)(2,1)S(1)}, bf16[512,1024]{1,0:T(8,128)...) custom-call(s32[7]{0:T(128)S(1)} %stack.88.idx_ref, ...), custom_call_target="tpu_custom_call" | custom-call | flops 7516192768 | bytes 16777216 | tf_op jit(solution)/shard_map/gradients/pallas_call | solution.py:346
  43.6 5.5 %collective-permute-done.10 = bf16[256,1024]{1,0:T(8,128)(2,1)S(1)} collective-permute-done((bf16[256,1024]{1,0:T(8,128)(2,1)}, bf16[256,1024]{1,0:T(8,128)(2,1)S(1)}, u32[]{:S(2)}, u32[]{:S(2)}) %collective-permute-start.10) | collective-permute-done | bytes 524320 | tf_op jit(solution)/shard_map/ppermute | solution.py:38
  50.2 1.4 collective-permute-start.16
  51.9 2.1 %collective-permute-start.14 = (bf16[512,1024]{1,0:T(8,128)(2,1)S(1)}, bf16[512,1024]{1,0:T(8,128)(2,1)S(1)}, u32[]{:S(2)}, u32[]{:S(2)}) collective-permute-start(bf16[512,1024]{1,0:T(8,128)(2,1)S(1)} %get-tuple-element.84.refs_6_), channel_id=1, source_target_pairs={{0,6},{1,7},{2,0},{3,1},{4,2},{5,3},{6,4},{7,5},{8,14},{9,15},{10,... | collective-permute-start | bytes 3145736 | tf_op jit(solution)/shard_map/ppermute | solution.py:42
  53.9 15.1 %forward.2 = (f32[512,1024]{1,0:T(8,128)S(1)}, f32[512,1024]{1,0:T(8,128)S(1)}, bf16[512,8192]{1,0:T(8,128)(2,1)}, bf16[4,512,512]{2,1,0:T(8,128)(2,1)}) custom-call(s32[4]{0:T(128)S(1)} %pad_add_fusion.idx_ref, bf16[512,8192]{1,0:T(8,128)(2,1)} %bitcast.34, bf16[7,512,512]{2,1,0:T(8,128)(2,1)} %collective-permute-done.8.oth_ref.refs_1_, ...), custom_call_target="tpu_custom_call" | custom-call | flops 8589934592 | bytes 20971520 | tf_op jit(solution)/shard_map/forward/pallas_call | solution.py:416
  69.1 2.1 %collective-permute-start.26 = (bf16[4,512,512]{2,1,0:T(8,128)(2,1)}, bf16[4,512,512]{2,1,0:T(8,128)(2,1)}, u32[]{:S(2)}, u32[]{:S(2)}) collective-permute-start(bf16[4,512,512]{2,1,0:T(8,128)(2,1)} %get-tuple-element.98), channel_id=1, source_target_pairs={{0,1},{1,0},{2,3},{3,2},{4,5},{5,4},{6,7},{7,6},{8,9},{9,8},{10,11... | collective-permute-start | bytes 6291464 | tf_op jit(solution)/shard_map/ppermute | solution.py:50
  71.2 3.1 %collective-permute-done.16 = bf16[512,1024]{1,0:T(8,128)(2,1)S(1)} collective-permute-done((bf16[512,1024]{1,0:T(8,128)(2,1)S(1)}, bf16[512,1024]{1,0:T(8,128)(2,1)S(1)}, u32[]{:S(2)}, u32[]{:S(2)}) %collective-permute-start.16) | collective-permute-done | bytes 1048608 | tf_op jit(solution)/shard_map/ppermute | solution.py:38
  74.3 1.4 add_convert_fusion.refs_4_
  75.7 1.7 add_convert_fusion.1.refs_3_
  77.4 1.6 collective-permute-start.18
  79.0 2.6 %collective-permute-start.15 = (bf16[512,1024]{1,0:T(8,128)(2,1)}, bf16[512,1024]{1,0:T(8,128)(2,1)}, u32[]{:S(2)}, u32[]{:S(2)}) collective-permute-start(bf16[512,1024]{1,0:T(8,128)(2,1)} %add_convert_fusion.1.refs_3_), channel_id=1, source_target_pairs={{0,6},{1,7},{2,0},{3,1},{4,2},{5,3},{6,4},{7,5},{8,14},{9,15},{10,... | collective-permute-start | bytes 3145736 | tf_op jit(solution)/shard_map/ppermute | solution.py:42
  82.3 22.1 %conditional.7 = (bf16[512,1024]{1,0:T(8,128)(2,1)}) conditional(s32[]{:T(128)} %clamp.4, bf16[512,1024]{1,0:T(8,128)(2,1)} %get-tuple-element.90, bf16[512,1024]{1,0:T(8,128)(2,1)} %get-tuple-element.90, bf16[512,1024]{1,0:T(8,128)(2,1)} %get-tuple-element.90), branch_computations={%region_0.1_spmd, %region_1.2_spmd, %region_2.3_spmd} | conditional | bytes 4194352 | solution.py:57
  82.3 1.3 collective-permute-start
  83.6 20.8 %collective-permute-done = bf16[512,1024]{1,0:T(8,128)(2,1)} collective-permute-done((bf16[512,1024]{1,0:T(8,128)(2,1)}, bf16[512,1024]{1,0:T(8,128)(2,1)}, u32[]{:S(2)}, u32[]{:S(2)}) %collective-permute-start) | collective-permute-done | bytes 1048608 | tf_op jit(solution)/shard_map/cond/branch_0_fun/ppermute | solution.py:55
  104.6 2.7 %collective-permute-start.21 = (bf16[512,1024]{1,0:T(8,128)(2,1)}, bf16[512,1024]{1,0:T(8,128)(2,1)}, u32[]{:S(2)}, u32[]{:S(2)}) collective-permute-start(bf16[512,1024]{1,0:T(8,128)(2,1)} %get-tuple-element.92), channel_id=1, source_target_pairs={{0,6},{1,7},{2,0},{3,1},{4,2},{5,3},{6,4},{7,5},{8,14},{9,15},{10,... | collective-permute-start | bytes 3145736 | tf_op jit(solution)/shard_map/ppermute | solution.py:42
  107.4 3.2 %unpack.2.refs_9_ = bf16[512,8192]{1,0:T(8,128)(2,1)} custom-call(s32[4]{0:T(128)S(1)} %pad_add_fusion.2.idx_ref, bf16[512,8192]{1,0:T(8,128)(2,1)} %get-tuple-element.97.old_ref, bf16[4,512,512]{2,1,0:T(8,128)(2,1)} %collective-permute-done.26.piece_ref), custom_call_target="tpu_custom_call", output_to_operand_aliasing={{}: (1, {})} | custom-call | bytes 4194304 | tf_op jit(solution)/shard_map/unpack/pallas_call | solution.py:217
  110.7 4.2 %fusion.4 = (bf16[512,1024]{1,0:T(8,128)(2,1)S(1)}, f32[512,1024]{1,0:T(8,128)}) fusion(bf16[512,1024]{1,0:T(8,128)(2,1)} %collective-permute-done.18.refs_4_, bf16[512,1024]{1,0:T(8,128)(2,1)} %collective-permute-done.15.refs_2_, bf16[512,1024]{1,0:T(8,128)(2,1)} %collective-permute-done.17.refs_3_, bf16[512,1024]{1,0:T(8,128)(2,1)S(1)} %copy-done.12, ...), kind=kLoop, calls=%fused_computation.18 | loop fusion | flops 5242880 | bytes 9437184 | tf_op jit(solution)/shard_map/convert_element_type | solution.py:543
  114.9 21.4 %conditional.9 = (bf16[512,1024]{1,0:T(8,128)(2,1)}, bf16[512,1024]{1,0:T(8,128)(2,1)S(1)}) conditional(s32[]{:T(128)} %clamp.4, bf16[512,1024]{1,0:T(8,128)(2,1)S(1)} %get-tuple-element.111, bf16[512,1024]{1,0:T(8,128)(2,1)S(1)} %get-tuple-element.111, bf16[512,1024]{1,0:T(8,128)(2,1)S(1)} %get-tuple-element.111), branch_computations={%region_3.4_spmd, %region_4.5_spmd, %region_5.6_spmd} | conditional | bytes 6291512
  114.9 1.2 collective-permute-start.3
  116.1 18.9 %collective-permute-done.3 = bf16[512,1024]{1,0:T(8,128)(2,1)} collective-permute-done((bf16[512,1024]{1,0:T(8,128)(2,1)S(1)}, bf16[512,1024]{1,0:T(8,128)(2,1)}, u32[]{:S(2)}, u32[]{:S(2)}) %collective-permute-start.3) | collective-permute-done | bytes 1048608 | tf_op jit(solution)/shard_map/cond/branch_0_fun/ppermute | solution.py:55
  135.1 1.2 copy.37
  136.3 1.4 slice.52.refs_4_
  137.8 1.0 slice.54.refs_6_
  138.8 1.4 collective-permute-start.24
  140.2 1.0 slice.53.refs_5_
  141.2 2.7 %collective-permute-start.22 = (bf16[160,1024]{1,0:T(8,128)(2,1)S(1)}, bf16[160,1024]{1,0:T(8,128)(2,1)S(1)}, u32[]{:S(2)}, u32[]{:S(2)}) collective-permute-start(bf16[160,1024]{1,0:T(8,128)(2,1)S(1)} %slice.53.refs_5_), channel_id=1, source_target_pairs={{0,6},{1,7},{2,0},{3,1},{4,2},{5,3},{6,4},{7,5},{8,14},{9,15},{10,... | collective-permute-start | bytes 983048 | tf_op jit(solution)/shard_map/ppermute | solution.py:42
  144.0 1.6 copy-done.8
  145.5 13.1 %forward.3 = (f32[512,1024]{1,0:T(8,128)S(1)}, bf16[512,1024]{1,0:T(8,128)(2,1)}, bf16[512,8192]{1,0:T(8,128)(2,1)}, bf16[3,512,512]{2,1,0:T(8,128)(2,1)S(1)}) custom-call(s32[3]{0:T(128)S(1)} %pad_add_fusion.1.idx_ref, bf16[512,8192]{1,0:T(8,128)(2,1)} %bitcast.35, ...), custom_call_target="tpu_custom_call", output_to_operand_aliasing={{2}: (14, {})} | custom-call | flops 6442450944 | bytes 17825792 | tf_op jit(solution)/shard_map/forward/pallas_call | solution.py:416
  158.7 6.5 %collective-permute-start.27 = (bf16[3,512,512]{2,1,0:T(8,128)(2,1)S(1)}, bf16[3,512,512]{2,1,0:T(8,128)(2,1)S(1)}, u32[]{:S(2)}, u32[]{:S(2)}) collective-permute-start(bf16[3,512,512]{2,1,0:T(8,128)(2,1)S(1)} %get-tuple-element.101), channel_id=1, source_target_pairs={{0,1},{1,0},{2,3},{3,2},{4,5},{5,4},{6,7},{7,6},{8,9},{9,8},{10,11... | collective-permute-start | bytes 4718600 | tf_op jit(solution)/shard_map/ppermute | solution.py:50
  165.2 2.0 %fusion = (f32[512,1024]{1,0:T(8,128)S(1)}, f32[512,1024]{1,0:T(8,128)S(1)}) fusion(f32[512,1024]{1,0:T(8,128)S(1)} %copy-done.14, bf16[512,1024]{1,0:T(8,128)(2,1)S(1)} %copy-done.16, bf16[512,1024]{1,0:T(8,128)(2,1)} %get-tuple-element.121.refs_5_, f32[1,512,1024]{2,1,0:T(8,128)S(1)} %copy-done.13), kind=kLoop, calls=%fused_computation.2 | loop fusion | flops 5242880 | bytes 10485760 | tf_op jit(solution)/shard_map/mul | solution.py:548
  167.3 0.7 collective-permute-start.28
  169.3 0.7 collective-permute-start.25
  170.1 1.8 %unpack.3.rest_0_ = bf16[512,8192]{1,0:T(8,128)(2,1)} custom-call(s32[3]{0:T(128)S(1)} %pad_add_fusion.3.idx_ref, bf16[512,8192]{1,0:T(8,128)(2,1)} %get-tuple-element.100.old_ref, bf16[3,512,512]{2,1,0:T(8,128)(2,1)S(1)} %collective-permute-done.27.piece_ref), custom_call_target="tpu_custom_call", output_to_operand_aliasing={{}: (1, {})} | custom-call | bytes 3145728 | tf_op jit(solution)/shard_map/unpack/pallas_call | solution.py:217
  171.9 1.1 slice-done.1
  173.6 2.3 %one_shard.2 = (f32[512,1024]{1,0:T(8,128)S(1)}, bf16[512,8192]{1,0:T(8,128)(2,1)}) custom-call(s32[1]{0:T(128)} %bitcast.18.idx_ref, bf16[512,8192]{1,0:T(8,128)(2,1)S(1)} %bitcast.38, bf16[512,1024]{1,0:T(8,128)(2,1)S(1)} %bitcast.45, bf16[512,1024]{1,0:T(8,128)(2,1)S(1)} %held_until.9.w_ref, ...), custom_call_target="tpu_custom_call", output_to_operand_aliasing={{1}: (5, {})} | custom-call | flops 1073741824 | bytes 8388608 | tf_op jit(solution)/shard_map/one_shard/pallas_call | solution.py:478
  175.9 2.4 %one_shard.3 = (bf16[512,1024]{1,0:T(8,128)(2,1)}, bf16[512,8192]{1,0:T(8,128)(2,1)}) custom-call(s32[1]{0:T(128)} %bitcast.idx_ref, bf16[512,8192]{1,0:T(8,128)(2,1)S(1)} %bitcast.39, bf16[512,1024]{1,0:T(8,128)(2,1)S(1)} %bitcast.46, bf16[512,1024]{1,0:T(8,128)(2,1)S(1)} %collective-permute-done.25.w_ref, ...), custom_call_target="tpu_custom_call", output_to_operand_aliasing={{1}: (6, {})} | custom-call | flops 1073741824 | bytes 8388608 | tf_op jit(solution)/shard_map/one_shard/pallas_call | solution.py:478
  (78 shorter events, 4.7 us)
Async XLA Ops:
  10.2 17.4 %collective-permute-start.8 = (bf16[7,512,512]{2,1,0:T(8,128)(2,1)}, bf16[7,512,512]{2,1,0:T(8,128)(2,1)}, u32[]{:S(2)}, u32[]{:S(2)}) collective-permute-start(bf16[7,512,512]{2,1,0:T(8,128)(2,1)} %pack.1), channel_id=1, source_target_pairs={{0,1},{1,0},{2,3},{3,2},{4,5},{5,4},{6,7},{7,6},{8,9},{9,8},{10,11... | collective-permute-start | bytes 11010056 | tf_op jit(solution)/shard_map/ppermute | solution.py:50
  11.7 8.4 %collective-permute-start.9 = (bf16[512,1536]{1,0:T(8,128)(2,1)}, bf16[512,1536]{1,0:T(8,128)(2,1)S(1)}, u32[]{:S(2)}, u32[]{:S(2)}) collective-permute-start(bf16[512,1536]{1,0:T(8,128)(2,1)} %pack_first.1.after_ref), channel_id=1, source_target_pairs={{0,1},{1,0},{2,3},{3,2},{4,5},{5,4},{6,7},{7,6},{8,9},{9,8},{10,11... | collective-permute-start | bytes 4718600 | tf_op jit(solution)/shard_map/ppermute | solution.py:50
  11.8 38.4 %collective-permute-start.6 = (bf16[512,1024]{1,0:T(8,128)(2,1)}, bf16[512,1024]{1,0:T(8,128)(2,1)}, u32[]{:S(2)}, u32[]{:S(2)}) collective-permute-start(bf16[512,1024]{1,0:T(8,128)(2,1)} %bitcast_convert_fusion.after_ref.refs_3_.refs_1_), channel_id=1, source_target_pairs={{0,2},{1,3},{2,4},{3,5},{4,6},{5,7},{6,0},{7,1},{8,10},{9,11},{10,... | collective-permute-start | bytes 3145736 | tf_op jit(solution)/shard_map/ppermute | solution.py:38
  13.2 37.0 %collective-permute-start.7 = (bf16[512,1024]{1,0:T(8,128)(2,1)}, bf16[512,1024]{1,0:T(8,128)(2,1)}, u32[]{:S(2)}, u32[]{:S(2)}) collective-permute-start(bf16[512,1024]{1,0:T(8,128)(2,1)} %bitcast_convert_fusion.after_ref.refs_3_.refs_1_), channel_id=1, source_target_pairs={{0,8},{1,9},{2,10},{3,11},{4,12},{5,13},{6,14},{7,15},{8,0},{9,1},... | collective-permute-start | bytes 3145736 | tf_op jit(solution)/shard_map/ppermute | solution.py:46
  14.8 35.4 %collective-permute-start.12 = (bf16[512,1024]{1,0:T(8,128)(2,1)}, bf16[512,1024]{1,0:T(8,128)(2,1)}, u32[]{:S(2)}, u32[]{:S(2)}) collective-permute-start(bf16[512,1024]{1,0:T(8,128)(2,1)} %bitcast_convert_fusion.after_ref.refs_3_.refs_1_), channel_id=1, source_target_pairs={{0,6},{1,7},{2,0},{3,1},{4,2},{5,3},{6,4},{7,5},{8,14},{9,15},{10,... | collective-permute-start | bytes 3145736 | tf_op jit(solution)/shard_map/ppermute | solution.py:42
  20.0 1.1 copy-start.1
  26.1 22.9 %collective-permute-start.10 = (bf16[256,1024]{1,0:T(8,128)(2,1)}, bf16[256,1024]{1,0:T(8,128)(2,1)S(1)}, u32[]{:S(2)}, u32[]{:S(2)}) collective-permute-start(bf16[256,1024]{1,0:T(8,128)(2,1)} %get-tuple-element.79), channel_id=1, source_target_pairs={{0,2},{1,3},{2,4},{3,5},{4,6},{5,7},{6,0},{7,1},{8,10},{9,11},{10,... | collective-permute-start | bytes 1572872 | tf_op jit(solution)/shard_map/ppermute | solution.py:38
  27.6 1.6 copy-start
  27.6 1.7 copy-start.2
  27.6 22.3 %collective-permute-start.11 = (bf16[256,1024]{1,0:T(8,128)(2,1)}, bf16[256,1024]{1,0:T(8,128)(2,1)S(1)}, u32[]{:S(2)}, u32[]{:S(2)}) collective-permute-start(bf16[256,1024]{1,0:T(8,128)(2,1)} %held_until.5), channel_id=1, source_target_pairs={{0,6},{1,7},{2,0},{3,1},{4,2},{5,3},{6,4},{7,5},{8,14},{9,15},{10,... | collective-permute-start | bytes 1572872 | tf_op jit(solution)/shard_map/ppermute | solution.py:42
  43.6 6.6 %copy-start.11 = (bf16[512,1024]{1,0:T(8,128)(2,1)}, bf16[512,1024]{1,0:T(8,128)(2,1)S(1)}, u32[]{:S(2)}) copy-start(bf16[512,1024]{1,0:T(8,128)(2,1)S(1)} %get-tuple-element.93) | copy-start | bytes 3145732
  50.2 24.1 %collective-permute-start.16 = (bf16[512,1024]{1,0:T(8,128)(2,1)S(1)}, bf16[512,1024]{1,0:T(8,128)(2,1)S(1)}, u32[]{:S(2)}, u32[]{:S(2)}) collective-permute-start(bf16[512,1024]{1,0:T(8,128)(2,1)S(1)} %get-tuple-element.86.refs_4_), channel_id=1, source_target_pairs={{0,2},{1,3},{2,4},{3,5},{4,6},{5,7},{6,0},{7,1},{8,10},{9,11},{10,... | collective-permute-start | bytes 3145736 | tf_op jit(solution)/shard_map/ppermute | solution.py:38
  51.6 24.1 %collective-permute-start.13 = (bf16[512,1024]{1,0:T(8,128)(2,1)S(1)}, bf16[512,1024]{1,0:T(8,128)(2,1)S(1)}, u32[]{:S(2)}, u32[]{:S(2)}) collective-permute-start(bf16[512,1024]{1,0:T(8,128)(2,1)S(1)} %get-tuple-element.83.refs_5_), channel_id=1, source_target_pairs={{0,8},{1,9},{2,10},{3,11},{4,12},{5,13},{6,14},{7,15},{8,0},{9,1},... | collective-permute-start | bytes 3145736 | tf_op jit(solution)/shard_map/ppermute | solution.py:46
  51.9 23.9 %collective-permute-start.14 = (bf16[512,1024]{1,0:T(8,128)(2,1)S(1)}, bf16[512,1024]{1,0:T(8,128)(2,1)S(1)}, u32[]{:S(2)}, u32[]{:S(2)}) collective-permute-start(bf16[512,1024]{1,0:T(8,128)(2,1)S(1)} %get-tuple-element.84.refs_6_), channel_id=1, source_target_pairs={{0,6},{1,7},{2,0},{3,1},{4,2},{5,3},{6,4},{7,5},{8,14},{9,15},{10,... | collective-permute-start | bytes 3145736 | tf_op jit(solution)/shard_map/ppermute | solution.py:42
  69.1 8.3 %copy-start.7 = (f32[512,1024]{1,0:T(8,128)}, f32[512,1024]{1,0:T(8,128)S(1)}, u32[]{:S(2)}) copy-start(f32[512,1024]{1,0:T(8,128)S(1)} %get-tuple-element.96.refs_8_) | copy-start | bytes 6291460
  69.1 8.3 %copy-start.3 = (f32[512,1024]{1,0:T(8,128)}, f32[512,1024]{1,0:T(8,128)S(1)}, u32[]{:S(2)}) copy-start(f32[512,1024]{1,0:T(8,128)S(1)} %get-tuple-element.87.refs_2_.refs_7_) | copy-start | bytes 6291460
  69.1 38.3 %collective-permute-start.26 = (bf16[4,512,512]{2,1,0:T(8,128)(2,1)}, bf16[4,512,512]{2,1,0:T(8,128)(2,1)}, u32[]{:S(2)}, u32[]{:S(2)}) collective-permute-start(bf16[4,512,512]{2,1,0:T(8,128)(2,1)} %get-tuple-element.98), channel_id=1, source_target_pairs={{0,1},{1,0},{2,3},{3,2},{4,5},{5,4},{6,7},{7,6},{8,9},{9,8},{10,11... | collective-permute-start | bytes 6291464 | tf_op jit(solution)/shard_map/ppermute | solution.py:50
  77.4 27.0 %collective-permute-start.17 = (bf16[512,1024]{1,0:T(8,128)(2,1)}, bf16[512,1024]{1,0:T(8,128)(2,1)}, u32[]{:S(2)}, u32[]{:S(2)}) collective-permute-start(bf16[512,1024]{1,0:T(8,128)(2,1)} %get-tuple-element.89), channel_id=1, source_target_pairs={{0,2},{1,3},{2,4},{3,5},{4,6},{5,7},{6,0},{7,1},{8,10},{9,11},{10,... | collective-permute-start | bytes 3145736 | tf_op jit(solution)/shard_map/ppermute | solution.py:38
  77.4 27.0 %collective-permute-start.18 = (bf16[512,1024]{1,0:T(8,128)(2,1)}, bf16[512,1024]{1,0:T(8,128)(2,1)}, u32[]{:S(2)}, u32[]{:S(2)}) collective-permute-start(bf16[512,1024]{1,0:T(8,128)(2,1)} %add_convert_fusion.refs_4_), channel_id=1, source_target_pairs={{0,8},{1,9},{2,10},{3,11},{4,12},{5,13},{6,14},{7,15},{8,0},{9,1},... | collective-permute-start | bytes 3145736 | tf_op jit(solution)/shard_map/ppermute | solution.py:46
  79.0 25.4 %collective-permute-start.15 = (bf16[512,1024]{1,0:T(8,128)(2,1)}, bf16[512,1024]{1,0:T(8,128)(2,1)}, u32[]{:S(2)}, u32[]{:S(2)}) collective-permute-start(bf16[512,1024]{1,0:T(8,128)(2,1)} %add_convert_fusion.1.refs_3_), channel_id=1, source_target_pairs={{0,6},{1,7},{2,0},{3,1},{4,2},{5,3},{6,4},{7,5},{8,14},{9,15},{10,... | collective-permute-start | bytes 3145736 | tf_op jit(solution)/shard_map/ppermute | solution.py:42
  82.3 22.1 %collective-permute-start = (bf16[512,1024]{1,0:T(8,128)(2,1)}, bf16[512,1024]{1,0:T(8,128)(2,1)}, u32[]{:S(2)}, u32[]{:S(2)}) collective-permute-start(bf16[512,1024]{1,0:T(8,128)(2,1)} %param.4), channel_id=1, source_target_pairs={{0,16},{16,0},{32,48},{48,32},{64,80},{80,64},{96,112},{112,96},{1... | collective-permute-start | bytes 3145736 | tf_op jit(solution)/shard_map/cond/branch_0_fun/ppermute | solution.py:55
  104.4 31.9 %collective-permute-start.19 = (bf16[512,1024]{1,0:T(8,128)(2,1)}, bf16[512,1024]{1,0:T(8,128)(2,1)}, u32[]{:S(2)}, u32[]{:S(2)}) collective-permute-start(bf16[512,1024]{1,0:T(8,128)(2,1)} %get-tuple-element.91), channel_id=1, source_target_pairs={{0,8},{1,9},{2,10},{3,11},{4,12},{5,13},{6,14},{7,15},{8,0},{9,1},... | collective-permute-start | bytes 3145736 | tf_op jit(solution)/shard_map/ppermute | solution.py:46
  104.5 33.3 %collective-permute-start.23 = (bf16[512,1024]{1,0:T(8,128)(2,1)}, bf16[512,1024]{1,0:T(8,128)(2,1)}, u32[]{:S(2)}, u32[]{:S(2)}) collective-permute-start(bf16[512,1024]{1,0:T(8,128)(2,1)} %get-tuple-element.91), channel_id=1, source_target_pairs={{0,2},{1,3},{2,4},{3,5},{4,6},{5,7},{6,0},{7,1},{8,10},{9,11},{10,... | collective-permute-start | bytes 3145736 | tf_op jit(solution)/shard_map/ppermute | solution.py:38
  104.6 35.6 %collective-permute-start.21 = (bf16[512,1024]{1,0:T(8,128)(2,1)}, bf16[512,1024]{1,0:T(8,128)(2,1)}, u32[]{:S(2)}, u32[]{:S(2)}) collective-permute-start(bf16[512,1024]{1,0:T(8,128)(2,1)} %get-tuple-element.92), channel_id=1, source_target_pairs={{0,6},{1,7},{2,0},{3,1},{4,2},{5,3},{6,4},{7,5},{8,14},{9,15},{10,... | collective-permute-start | bytes 3145736 | tf_op jit(solution)/shard_map/ppermute | solution.py:42
  107.4 3.3 %copy-start.12 = (bf16[512,1024]{1,0:T(8,128)(2,1)S(1)}, bf16[512,1024]{1,0:T(8,128)(2,1)}, u32[]{:S(2)}) copy-start(bf16[512,1024]{1,0:T(8,128)(2,1)} %copy-done.11) | copy-start | bytes 3145732
  107.4 3.3 %copy-start.17 = (f32[1,512,1024]{2,1,0:T(8,128)S(1)}, f32[1,512,1024]{2,1,0:T(8,128)}, u32[]{:S(2)}) copy-start(f32[1,512,1024]{2,1,0:T(8,128)} %param.19) | copy-start | bytes 6291460
  114.9 20.1 %collective-permute-start.3 = (bf16[512,1024]{1,0:T(8,128)(2,1)S(1)}, bf16[512,1024]{1,0:T(8,128)(2,1)}, u32[]{:S(2)}, u32[]{:S(2)}) collective-permute-start(bf16[512,1024]{1,0:T(8,128)(2,1)S(1)} %param.7), channel_id=1, source_target_pairs={{0,16},{16,0},{32,48},{48,32},{64,80},{80,64},{96,112},{112,96},{1... | collective-permute-start | bytes 3145736 | tf_op jit(solution)/shard_map/cond/branch_0_fun/ppermute | solution.py:55
  136.3 7.7 %copy-start.15 = (bf16[512,1024]{1,0:T(8,128)(2,1)}, bf16[512,1024]{1,0:T(8,128)(2,1)S(1)}, u32[]{:S(2)}) copy-start(bf16[512,1024]{1,0:T(8,128)(2,1)S(1)} %get-tuple-element.110) | copy-start | bytes 3145732
  136.3 7.7 %copy-start.4 = (f32[512,1024]{1,0:T(8,128)S(1)}, f32[512,1024]{1,0:T(8,128)}, u32[]{:S(2)}) copy-start(f32[512,1024]{1,0:T(8,128)} %copy-done.3) | copy-start | bytes 6291460
  137.7 30.3 %collective-permute-start.20 = (bf16[176,1024]{1,0:T(8,128)(2,1)S(1)}, bf16[176,1024]{1,0:T(8,128)(2,1)S(1)}, u32[]{:S(2)}, u32[]{:S(2)}) collective-permute-start(bf16[176,1024]{1,0:T(8,128)(2,1)S(1)} %slice.52.refs_4_), channel_id=1, source_target_pairs={{0,2},{1,3},{2,4},{3,5},{4,6},{5,7},{6,0},{7,1},{8,10},{9,11},{10,... | collective-permute-start | bytes 1081352 | tf_op jit(solution)/shard_map/ppermute | solution.py:38
  138.8 29.2 %collective-permute-start.24 = (bf16[176,1024]{1,0:T(8,128)(2,1)S(1)}, bf16[176,1024]{1,0:T(8,128)(2,1)S(1)}, u32[]{:S(2)}, u32[]{:S(2)}) collective-permute-start(bf16[176,1024]{1,0:T(8,128)(2,1)S(1)} %slice.54.refs_6_), channel_id=1, source_target_pairs={{0,8},{1,9},{2,10},{3,11},{4,12},{5,13},{6,14},{7,15},{8,0},{9,1},... | collective-permute-start | bytes 1081352 | tf_op jit(solution)/shard_map/ppermute | solution.py:46
  141.2 26.8 %collective-permute-start.22 = (bf16[160,1024]{1,0:T(8,128)(2,1)S(1)}, bf16[160,1024]{1,0:T(8,128)(2,1)S(1)}, u32[]{:S(2)}, u32[]{:S(2)}) collective-permute-start(bf16[160,1024]{1,0:T(8,128)(2,1)S(1)} %slice.53.refs_5_), channel_id=1, source_target_pairs={{0,6},{1,7},{2,0},{3,1},{4,2},{5,3},{6,4},{7,5},{8,14},{9,15},{10,... | collective-permute-start | bytes 983048 | tf_op jit(solution)/shard_map/ppermute | solution.py:42
  143.9 1.6 copy-start.8
  145.5 19.7 %copy-start.13 = (f32[1,512,1024]{2,1,0:T(8,128)S(1)}, f32[1,512,1024]{2,1,0:T(8,128)}, u32[]{:S(2)}) copy-start(f32[1,512,1024]{2,1,0:T(8,128)} %param.18) | copy-start | bytes 6291460
  145.5 19.7 %copy-start.14 = (f32[512,1024]{1,0:T(8,128)S(1)}, f32[512,1024]{1,0:T(8,128)}, u32[]{:S(2)}) copy-start(f32[512,1024]{1,0:T(8,128)} %get-tuple-element.112) | copy-start | bytes 6291460
  145.5 19.7 %copy-start.16 = (bf16[512,1024]{1,0:T(8,128)(2,1)S(1)}, bf16[512,1024]{1,0:T(8,128)(2,1)}, u32[]{:S(2)}) copy-start(bf16[512,1024]{1,0:T(8,128)(2,1)} %copy-done.15) | copy-start | bytes 3145732
  158.7 8.6 %copy-start.9 = (f32[512,1024]{1,0:T(8,128)}, f32[512,1024]{1,0:T(8,128)S(1)}, u32[]{:S(2)}) copy-start(f32[512,1024]{1,0:T(8,128)S(1)} %get-tuple-element.99.key_ref) | copy-start | bytes 6291460
  158.7 11.4 %collective-permute-start.27 = (bf16[3,512,512]{2,1,0:T(8,128)(2,1)S(1)}, bf16[3,512,512]{2,1,0:T(8,128)(2,1)S(1)}, u32[]{:S(2)}, u32[]{:S(2)}) collective-permute-start(bf16[3,512,512]{2,1,0:T(8,128)(2,1)S(1)} %get-tuple-element.101), channel_id=1, source_target_pairs={{0,1},{1,0},{2,3},{3,2},{4,5},{5,4},{6,7},{7,6},{8,9},{9,8},{10,11... | collective-permute-start | bytes 4718600 | tf_op jit(solution)/shard_map/ppermute | solution.py:50
  167.3 1.3 copy-start.5
  167.3 2.0 %copy-start.6 = (f32[512,1024]{1,0:T(8,128)}, f32[512,1024]{1,0:T(8,128)S(1)}, u32[]{:S(2)}) copy-start(f32[512,1024]{1,0:T(8,128)S(1)} %get-tuple-element.114.refs_1_) | copy-start | bytes 6291460
  167.3 8.6 %collective-permute-start.28 = (bf16[512,1024]{1,0:T(8,128)(2,1)}, bf16[512,1024]{1,0:T(8,128)(2,1)S(1)}, u32[]{:S(2)}, u32[]{:S(2)}) collective-permute-start(bf16[512,1024]{1,0:T(8,128)(2,1)} %get-tuple-element.103), channel_id=1, source_target_pairs={{0,1},{1,0},{2,3},{3,2},{4,5},{5,4},{6,7},{7,6},{8,9},{9,8},{10,11... | collective-permute-start | bytes 3145736 | tf_op jit(solution)/shard_map/ppermute | solution.py:50
  168.1 3.8 %slice-start = ((s8[8388608]{0:T(1024)(128)(4,1)}), s8[4194304]{0:T(1024)(128)(4,1)S(1)}, s32[]{:S(2)}) async-start(s8[8388608]{0:T(1024)(128)(4,1)} %bitcast.36), calls=%async_computation | async-start | bytes 8388608
  169.3 6.6 %collective-permute-start.25 = (bf16[512,1024]{1,0:T(8,128)(2,1)S(1)}, bf16[512,1024]{1,0:T(8,128)(2,1)S(1)}, u32[]{:S(2)}, u32[]{:S(2)}) collective-permute-start(bf16[512,1024]{1,0:T(8,128)(2,1)S(1)} %held_until.9.w_ref), channel_id=1, source_target_pairs={{0,1},{1,0},{2,3},{3,2},{4,5},{5,4},{6,7},{7,6},{8,9},{9,8},{10,11... | collective-permute-start | bytes 3145736 | tf_op jit(solution)/shard_map/ppermute | solution.py:50
  170.0 3.0 %slice-start.1 = ((s8[8388608]{0:T(1024)(128)(4,1)}), s8[4194304]{0:T(1024)(128)(4,1)S(1)}, s32[]{:S(2)}) async-start(s8[8388608]{0:T(1024)(128)(4,1)} %bitcast.36), calls=%async_computation.1 | async-start | bytes 8388608
  170.0 3.6 %copy-start.10 = (f32[512,1024]{1,0:T(8,128)S(1)}, f32[512,1024]{1,0:T(8,128)}, u32[]{:S(2)}) copy-start(f32[512,1024]{1,0:T(8,128)} %copy-done.9) | copy-start | bytes 6291460
where the time goes:
time: 179 us; the launch traced here: 178 us
  Pallas kernels  63.2 us (35%)
  waiting for transfers between devices  52.8 us (29%)
  starting transfers between devices  36.5 us (20%)
  other arithmetic  12.9 us (7%)
  local copies, waits for them, and re-layouts  11.1 us (6%)
  between operations  2 us (1%)
    ppermute x2, waiting for transfers between devices, swap(): lax.ppermute(arr, 'rep', [(r, r ^ 1 << level) for r in range(1 << LEVELS)])  39.7 us
    pallas_call x2, Pallas kernels, forward(): pl.pallas_call(kernel, grid_spec=pltpu.PrefetchScalarGridSpec(num_scalar_...  28.2 us
    pallas_call x2, Pallas kernels, gradients(): pl.pallas_call(kernel, grid_spec=pltpu.PrefetchScalarGridSpec(num_scalar_...  19.2 us
    ppermute x6, starting transfers between devices, y_down(): return lax.ppermute(value, 'fsdp', shift(dy=-1))  13 us
    ppermute x6, starting transfers between devices, core_swap(): return lax.ppermute(value, 'fsdp', shift(dc=1))  11.7 us
    ppermute x6, waiting for transfers between devices, y_up(): return lax.ppermute(value, 'fsdp', shift(dy=1))  8.62 us
    unnamed x41, local copies, waits for them, and re-layouts  7.02 us
    pallas_call x2, Pallas kernels, unpack(): pl.pallas_call(kernel, grid_spec=pltpu.PrefetchScalarGridSpec(num_scalar_...  5.09 us
  transfers between devices with their start and end apart: 25, of which 6 were waited for; matrix products, arithmetic and copies ran while one was open for 8% of the time, Pallas kernels for 31%

commit v1 on v0

--- a/solution.py
+++ b/solution.py
@@ -75,8 +75,8 @@
     return pl.BlockSpec((ROWS, ROWS), lambda k, idx: (0, idx[k]))
 
 
-def by_step(start=0):
-    return pl.BlockSpec((1, ROWS, ROWS), lambda k, idx: (k + start, 0, 0))
+def by_step():
+    return pl.BlockSpec((1, ROWS, ROWS), lambda k, idx: (k, 0, 0))
 
 
 def params_of(flops, nbytes, vmem=36):
@@ -169,38 +169,6 @@
     )(idx, tokens, cot, after)
 
 
-def pack(tokens, idx, after):
-    n = idx.shape[0]
-
-    def kernel(idx_ref, tok_ref, after_ref, out_ref, buf, sem, out_sem):
-        del after_ref
-        through(
-            [
-                pltpu.make_async_copy(tok_ref.at[:, slab(idx_ref, k)], buf.at[k], sem.at[k])
-                for k in range(n)
-            ],
-            [pltpu.make_async_copy(buf.at[k], out_ref.at[k], out_sem.at[k]) for k in range(n)],
-        )
-
-    return pl.pallas_call(
-        kernel,
-        grid_spec=pltpu.PrefetchScalarGridSpec(
-            num_scalar_prefetch=1,
-            grid=(1,),
-            in_specs=[IN_HBM, ANYWHERE],
-            out_specs=ANYWHERE,
-            scratch_shapes=[
-                pltpu.VMEM((n, ROWS, ROWS), BF16),
-                pltpu.SemaphoreType.DMA((n,)),
-                pltpu.SemaphoreType.DMA((n,)),
-            ],
-        ),
-        out_shape=jax.ShapeDtypeStruct((n, ROWS, ROWS), BF16),
-        name="pack",
-        **params_of(0, n * 2**20, 58),
-    )(idx, tokens, after)
-
-
 def unpack(target, pieces, idx):
     n = idx.shape[0]
 
@@ -234,70 +202,6 @@
     )(idx, target, pieces)
 
 
-def cut_rows(parts):
-    n = len(parts)
-
-    def kernel(*refs):
-        ins, outs, (buf, sem, out_sem) = refs[:n], refs[n : 2 * n], refs[2 * n :]
-        spans = [pl.ds(lo, hi - lo) for _, lo, hi in parts]
-        through(
-            [
-                pltpu.make_async_copy(r.at[d], buf.at[d], sem.at[i])
-                for i, (r, d) in enumerate(zip(ins, spans))
-            ],
-            [
-                pltpu.make_async_copy(buf.at[d], r, out_sem.at[i])
-                for i, (r, d) in enumerate(zip(outs, spans))
-            ],
-        )
-
-    return pl.pallas_call(
-        kernel,
-        in_specs=[ANYWHERE] * n,
-        out_specs=[ANYWHERE] * n,
-        out_shape=[jax.ShapeDtypeStruct((hi - lo, KV), BF16) for _, lo, hi in parts],
-        scratch_shapes=[
-            pltpu.VMEM((ROWS, KV), BF16),
-            pltpu.SemaphoreType.DMA((n,)),
-            pltpu.SemaphoreType.DMA((n,)),
-        ],
-        name="cut_rows",
-        **params_of(0, 2 * 2**20),
-    )(*[array for array, _, _ in parts])
-
-
-def join_rows(pieces, bounds, after):
-    n, m = len(pieces), len(after)
-
-    def kernel(*refs):
-        ins, out, (buf, sem, out_sem) = refs[:n], refs[n + m], refs[n + m + 1 :]
-        spans = [pl.ds(lo, hi - lo) for lo, hi in bounds]
-        through(
-            [
-                pltpu.make_async_copy(r, buf.at[d], sem.at[i])
-                for i, (r, d) in enumerate(zip(ins, spans))
-            ],
-            [
-                pltpu.make_async_copy(buf.at[d], out.at[d], out_sem.at[i])
-                for i, d in enumerate(spans)
-            ],
-        )
-
-    return pl.pallas_call(
-        kernel,
-        in_specs=[ANYWHERE] * (n + m),
-        out_specs=ANYWHERE,
-        out_shape=jax.ShapeDtypeStruct((ROWS, KV), BF16),
-        scratch_shapes=[
-            pltpu.VMEM((ROWS, KV), BF16),
-            pltpu.SemaphoreType.DMA((n,)),
-            pltpu.SemaphoreType.DMA((n,)),
-        ],
-        name="join_rows",
-        **params_of(0, 2 * 2**20),
-    )(*pieces, *after)
-
-
 def held_until(values, after):
     n, m = len(values), len(after)
 
@@ -315,7 +219,7 @@
     )(*values, *after)
 
 
-def gradients(tokens, other_tokens, cot, first, idx, start=0, cuts=None, after=()):
+def gradients(tokens, other_tokens, cot, first, idx, cuts=None, after=()):
     n = idx.shape[0]
     if cuts is None:
         shapes = [(ROWS, KV)] * n
@@ -323,10 +227,11 @@
         shapes = [(hi - lo, KV) for lo, hi in cuts]
 
     def kernel(idx_ref, tok_ref, oth_ref, cot_ref, cot_oth_ref, *outs):
-        *outs, tok_buf, tok_sem = outs[len(after) :]
-        tok = token_slabs(idx_ref, tok_ref, tok_buf, tok_sem, n)
+        outs = outs[len(after) :]
+        outs, scratch = outs[: len(shapes)], outs[len(shapes) :]
+        tok = token_slabs(idx_ref, tok_ref, *scratch[:2], n)
         step = pl.program_id(0)
-        oth = oth_ref[...] if cuts is not None else oth_ref[0]
+        oth = oth_ref[...] if cuts is not None else token_slabs(idx_ref, oth_ref, *scratch[2:], n)
         total = dot(tok, cot_ref[...], TN) + dot(oth, cot_oth_ref[...], TN)
         total = (total * SCALE).astype(BF16)
         if cuts is not None:
@@ -342,7 +247,7 @@
     if cuts is not None:
         oth_spec = pl.BlockSpec((ROWS, ROWS), lambda k, idx: (0, KV // ROWS))
     else:
-        oth_spec = by_step(start)
+        oth_spec = IN_HBM
     return pl.pallas_call(
         kernel,
         grid_spec=pltpu.PrefetchScalarGridSpec(
@@ -351,7 +256,7 @@
             in_specs=[IN_HBM, oth_spec, whole((ROWS, KV)), whole((ROWS, KV))]
             + [ANYWHERE] * len(after),
             out_specs=[whole(s) for s in shapes],
-            scratch_shapes=slab_scratch(n),
+            scratch_shapes=slab_scratch(n) * (1 if cuts is not None else 2),
         ),
         out_shape=[jax.ShapeDtypeStruct(s, BF16) for s in shapes],
         name="gradients",
@@ -359,7 +264,7 @@
     )(idx, tokens, other_tokens, cot, first, *after)
 
 
-def forward(tokens, other_tokens, cot, first, weights, idx, start, after, keys=None, grad_in=None):
+def forward(tokens, other_tokens, cot, first, weights, idx, after, keys=None, grad_in=None):
     n, m = idx.shape[0], len(after)
     last = keys is not None
 
@@ -370,7 +275,7 @@
         else:
             own_out, oth_out, gi_ref, back_ref, *rest = rest
             acc = oth_out
-        w_buf, sem, tok_buf, tok_sem = rest
+        w_buf, sem, *slabs = rest
         step = pl.program_id(0)
 
         @pl.when(step == 0)
@@ -391,9 +296,10 @@
                 pltpu.make_async_copy(w_ref, w_buf.at[i], sem.at[i]).wait()
 
         w = w_buf[step]
-        tok = token_slabs(idx_ref, tok_ref, tok_buf, tok_sem, n)
+        tok = token_slabs(idx_ref, tok_ref, *slabs[:2], n)
+        oth = token_slabs(idx_ref, oth_ref, *slabs[2:], n)
         own_out[...] += dot(tok, w, NN)
-        acc[...] += dot(oth_ref[0], w, NN)
+        acc[...] += dot(oth, w, NN)
         gi_ref[...] = (dot(cot_ref[...], w, NT) * SCALE).astype(BF16)
         back_ref[0] = (dot(cot_oth_ref[...], w, NT) * SCALE).astype(BF16)
 
@@ -403,11 +309,11 @@
             def _():
                 oth_out[...] = (acc[...] * SCALE).astype(BF16)
 
-    in_specs = [IN_HBM, by_step(start), whole((ROWS, KV)), whole((ROWS, KV))]
+    in_specs = [IN_HBM, IN_HBM, whole((ROWS, KV)), whole((ROWS, KV))]
     in_specs += [ANYWHERE] * (n + m)
     operands = [tokens, other_tokens, cot, first, *weights, *after]
     aliases = {}
-    scratch = [pltpu.VMEM((n, ROWS, KV), BF16), pltpu.SemaphoreType.DMA((n,)), *slab_scratch(n)]
+    scratch = [pltpu.VMEM((n, ROWS, KV), BF16), pltpu.SemaphoreType.DMA((n,)), *slab_scratch(n) * 2]
     if last:
         in_specs += [whole((ROWS, KV))] * 2 + [ANYWHERE]
         operands += [*keys, grad_in]
@@ -502,19 +408,19 @@
 def body(round_index, tokens, cotangent, params, momentum):
     tokens, cot, params, momentum = tokens[0], cotangent[0], params[0], momentum[0]
     bit = jnp.mod(round_index, LEVELS)
-    half, cut, end = ROWS // 2, 176, 336
+    half = ROWS // 2
     core = lax.axis_index("fsdp").astype(jnp.int32) % NC
     far, far_oth = columns(FAR, core), columns(FAR, 1 - core)
     mid, mid_oth = columns(MIDDLE, core), columns(MIDDLE, 1 - core)
     near, near_oth = columns(NEAR, core), columns(NEAR, 1 - core)
-    rest, rest_oth = columns(MIDDLE + NEAR, core), columns(MIDDLE + NEAR, 1 - core)
+    rest = columns(MIDDLE + NEAR, core)
 
     own = params.astype(BF16)
     w_0m, w_01, w_10 = y_up(own), y_down(own), z_across(own)
 
     packed = pack_first(tokens, cot, far_oth, own)
     first = core_swap(packed)
-    others = core_swap(pack(tokens, rest_oth, packed))
+    others = core_swap(tokens)
 
     t0, t1 = gradients(tokens, first, cot, first, far, cuts=((0, half), (half, ROWS)))
     (t1,) = held_until((t1,), (others,))
@@ -526,7 +432,7 @@
     p_1m = p_1m.at[half:].add(t1)
     p_11, p_1m, p_02 = held_until((p_11, p_1m, p_02), (w_0m, w_01, w_10))
     key_own, key_oth, grad_in, back = forward(
-        tokens, others, cot, first, (w_0m, w_01, w_10, own), near, len(MIDDLE), (p_11, p_1m, p_02)
+        tokens, others, cot, first, (w_0m, w_01, w_10, own), near, (p_11, p_1m, p_02)
     )
     p_11, p_1m, p_02 = y_up(p_11), z_across(p_1m), y_down(p_02)
     p_0m = (p_0m.astype(F32) + p_1m.astype(F32) + p_02.astype(F32)).astype(BF16)
@@ -540,10 +446,10 @@
     grad_in = unpack(grad_in, core_swap(back), near_oth)
     w_0m, w_10 = held_until((w_0m, w_10), (p_0m, p_01, p_10, partner_params))
     w_02, w_11, w_1m = y_up(w_0m), y_down(w_10), z_across(w_0m)
-    partner_moved = partner_swap(moved.astype(BF16), bit)
-    bounds = (0, cut), (cut, end), (end, ROWS)
-    pieces = [w[lo:hi] for w, (lo, hi) in zip((w_1m, w_11, w_02), bounds)]
-    thirds = y_up(pieces[0]), y_down(pieces[1]), z_across(pieces[2])
+    (moved_sent,) = held_until((moved.astype(BF16),), (grad_in,))
+    partner_moved = partner_swap(moved_sent, bit)
+    pieces = w_1m[:half], w_11[half:]
+    halves = y_up(pieces[0]), y_down(pieces[1])
     theirs = partner_moved.astype(F32)
     new_momentum = 0.5 * (moved + theirs)
     partner_stepped = partner_params.astype(F32) - 0.1 * theirs
@@ -555,13 +461,12 @@
         first,
         (w_11, w_1m, w_02),
         mid,
-        0,
         (partner_moved, *pieces),
         (key_own, key_oth),
         grad_in,
     )
     key_oth = core_swap(key_oth)
-    (w_12,) = held_until((jnp.concatenate(thirds, axis=0),), (new_params, new_momentum))
+    (w_12,) = held_until((jnp.concatenate(halves, axis=0),), (new_params, new_momentum))
     w_12_oth = core_swap(w_12)
     grad_in = unpack(grad_in, core_swap(back), mid_oth)
     key_own, grad_in = one_shard(tokens, cot, w_12, key_own, grad_in, far)

time: 179 us -> 180 us (level)
  local copies, waits for them, and re-layouts: 11.1 us -> 18.2 us
  starting transfers between devices: 36.5 us -> 33.5 us
  waiting for transfers between devices: 52.8 us -> 50 us
    unnamed x41 -> x43, local copies, waits for them, and re-layouts: 7.02 us -> 15.5 us
    ppermute x6, waiting for transfers between devices: 8.62 us -> 3.96 us  [y_up(): return lax.ppermute(value, 'fsdp', shift(dy=1))]
    pallas_call x1 -> x0, Pallas kernels: 3.78 us -> none  [pack(): pl.pallas_call(kernel, grid_spec=pltpu.PrefetchScalarGridSpec(num_scalar_...]
    ppermute x6, starting transfers between devices: 13 us -> 9.88 us  [y_down(): return lax.ppermute(value, 'fsdp', shift(dy=-1))]
    ppermute x6, starting transfers between devices: 4.35 us -> 6.26 us  [y_up(): return lax.ppermute(value, 'fsdp', shift(dy=1))]
    ppermute x5 -> x4, starting transfers between devices: 4.93 us -> 3.57 us  [z_across(): return lax.ppermute(value, 'fsdp', shift(dz=1))]
  transfers between devices with their start and end apart: 25 -> 24, of which waited for: 6 -> 6; matrix products, arithmetic and copies ran while one was open for 8% -> 10% of each run, Pallas kernels for 31% -> 32%
where the time goes in v1:
time: 180 us; the launch traced here: 179 us
  Pallas kernels  61.8 us (34%)
  waiting for transfers between devices  50 us (28%)
  starting transfers between devices  33.5 us (19%)
  local copies, waits for them, and re-layouts  18.2 us (10%)
  other arithmetic  14 us (8%)
    ppermute x2, waiting for transfers between devices, swap(): lax.ppermute(arr, 'rep', [(r, r ^ 1 << level) for r in range(1 << LEVELS)])  39.8 us
    pallas_call x2, Pallas kernels, forward(): pl.pallas_call(kernel, grid_spec=pltpu.PrefetchScalarGridSpec(num_scalar_...  28.8 us
    pallas_call x2, Pallas kernels, gradients(): pl.pallas_call(kernel, grid_spec=pltpu.PrefetchScalarGridSpec(num_scalar_...  19 us
    unnamed x43, local copies, waits for them, and re-layouts  15.5 us
    ppermute x6, starting transfers between devices, core_swap(): return lax.ppermute(value, 'fsdp', shift(dc=1))  11.4 us
    ppermute x6, starting transfers between devices, y_down(): return lax.ppermute(value, 'fsdp', shift(dy=-1))  9.88 us
    ppermute x6, starting transfers between devices, y_up(): return lax.ppermute(value, 'fsdp', shift(dy=1))  6.26 us
    pallas_call x2, Pallas kernels, unpack(): pl.pallas_call(kernel, grid_spec=pltpu.PrefetchScalarGridSpec(num_scalar_...  6 us
  transfers between devices with their start and end apart: 24, of which 6 were waited for; matrix products, arithmetic and copies ran while one was open for 10% of the time, Pallas kernels for 32%

profile of v1, /device:TPU:1, one launch (start us, length us, event | category | flops | bytes accessed | tf_op | source)
XLA Modules:
  0.0 179.3 jit_solution(18370680762686359485)
XLA Ops:
  0.6 1.5 collective-permute-start.8
  2.1 2.7 %bitcast_convert_fusion.after_ref.refs_3_.refs_1_ = bf16[512,1024]{1,0:T(8,128)(2,1)} fusion(f32[1,512,1024]{2,1,0:T(8,128)} %param.18), kind=kLoop, calls=%fused_computation.8 | loop fusion | flops 524288 | bytes 3145728 | tf_op jit(solution)/shard_map/convert_element_type | solution.py:418
  4.9 2.2 %pack_first.1 = bf16[512,1536]{1,0:T(8,128)(2,1)} custom-call(s32[1]{0:T(128)} %bitcast.idx_ref, bf16[512,8192]{1,0:T(8,128)(2,1)} %bitcast.32, bf16[512,1024]{1,0:T(8,128)(2,1)} %bitcast.41, bf16[512,1024]{1,0:T(8,128)(2,1)} %bitcast_convert_fusion.after_ref.refs_3_.refs_1_), custom_call_target="tpu_custom_call" | custom-call | bytes 3145728 | tf_op jit(solution)/shard_map/pack_first/pallas_call | solution.py:153
  7.3 1.4 collective-permute-start.6
  8.7 1.6 collective-permute-start.7
  10.3 1.5 collective-permute-start.12
  11.9 5.5 %collective-permute-done.9.cot_oth_ref.oth_ref = bf16[512,1536]{1,0:T(8,128)(2,1)S(1)} collective-permute-done((bf16[512,1536]{1,0:T(8,128)(2,1)}, bf16[512,1536]{1,0:T(8,128)(2,1)S(1)}, u32[]{:S(2)}, u32[]{:S(2)}) %collective-permute-start.9) | collective-permute-done | bytes 1572896 | tf_op jit(solution)/shard_map/ppermute | solution.py:50
  17.4 1.1 copy-done.4
  18.5 5.0 %gradients.3 = (bf16[256,1024]{1,0:T(8,128)(2,1)}, bf16[256,1024]{1,0:T(8,128)(2,1)}) custom-call(s32[1]{0:T(128)} %bitcast.11.idx_ref, bf16[512,8192]{1,0:T(8,128)(2,1)} %bitcast.33, bf16[512,1536]{1,0:T(8,128)(2,1)} %copy-done.4, bf16[512,1024]{1,0:T(8,128)(2,1)} %bitcast.42, bf16[512,1536]{1,0:T(8,128)(2,1)} %copy-done.4), custom_call_target="tpu_custom_call" | custom-call | flops 1073741824 | bytes 4194304 | tf_op jit(solution)/shard_map/gradients/pallas_call | solution.py:251
  23.5 1.4 collective-permute-start.10
  24.9 1.6 collective-permute-start.11
  26.7 3.4 %copy-done.1 = bf16[1,512,8192]{2,1,0:T(8,128)(2,1)S(1)} copy-done((bf16[1,512,8192]{2,1,0:T(8,128)(2,1)S(1)}, bf16[1,512,8192]{2,1,0:T(8,128)(2,1)}, u32[]{:S(2)}) %copy-start.1) | copy-done | bytes 8388632
  30.1 14.0 %gradients.2 = (bf16[512,1024]{1,0:T(8,128)(2,1)S(1)}, bf16[512,1024]{1,0:T(8,128)(2,1)S(1)}, bf16[512,1024]{1,0:T(8,128)(2,1)S(1)}, bf16[512,1024]{1,0:T(8,128)...) custom-call(s32[7]{0:T(128)S(1)} %stack.78.idx_ref, ...), custom_call_target="tpu_custom_call" | custom-call | flops 7516192768 | bytes 16777216 | tf_op jit(solution)/shard_map/gradients/pallas_call | solution.py:251
  45.7 1.4 collective-permute-start.16
  47.2 1.0 collective-permute-start.13
  48.1 1.4 collective-permute-start.14
  49.5 15.1 %forward.2 = (f32[512,1024]{1,0:T(8,128)S(1)}, f32[512,1024]{1,0:T(8,128)S(1)}, bf16[512,8192]{1,0:T(8,128)(2,1)}, bf16[4,512,512]{2,1,0:T(8,128)(2,1)}) custom-call(s32[4]{0:T(128)S(1)} %pad_add_fusion.idx_ref, bf16[512,8192]{1,0:T(8,128)(2,1)} %bitcast.34, bf16[512,8192]{1,0:T(8,128)(2,1)} %collective-permute-done.8.oth_ref.refs_1_, ...), custom_call_target="tpu_custom_call" | custom-call | flops 8589934592 | bytes 20971520 | tf_op jit(solution)/shard_map/forward/pallas_call | solution.py:322
  64.7 2.0 %collective-permute-start.23 = (bf16[4,512,512]{2,1,0:T(8,128)(2,1)}, bf16[4,512,512]{2,1,0:T(8,128)(2,1)}, u32[]{:S(2)}, u32[]{:S(2)}) collective-permute-start(bf16[4,512,512]{2,1,0:T(8,128)(2,1)} %get-tuple-element.95), channel_id=1, source_target_pairs={{0,1},{1,0},{2,3},{3,2},{4,5},{5,4},{6,7},{7,6},{8,9},{9,8},{10,11... | collective-permute-start | bytes 6291464 | tf_op jit(solution)/shard_map/ppermute | solution.py:50
  66.7 3.4 %collective-permute-done.16 = bf16[512,1024]{1,0:T(8,128)(2,1)S(1)} collective-permute-done((bf16[512,1024]{1,0:T(8,128)(2,1)S(1)}, bf16[512,1024]{1,0:T(8,128)(2,1)S(1)}, u32[]{:S(2)}, u32[]{:S(2)}) %collective-permute-start.16) | collective-permute-done | bytes 1048608 | tf_op jit(solution)/shard_map/ppermute | solution.py:38
  70.1 1.4 add_convert_fusion.refs_4_
  71.5 1.6 add_convert_fusion.1.refs_3_
  73.2 0.8 collective-permute-start.17
  73.9 0.9 collective-permute-start.18
  74.8 2.4 %collective-permute-start.15 = (bf16[512,1024]{1,0:T(8,128)(2,1)}, bf16[512,1024]{1,0:T(8,128)(2,1)}, u32[]{:S(2)}, u32[]{:S(2)}) collective-permute-start(bf16[512,1024]{1,0:T(8,128)(2,1)} %add_convert_fusion.1.refs_3_), channel_id=1, source_target_pairs={{0,6},{1,7},{2,0},{3,1},{4,2},{5,3},{6,4},{7,5},{8,14},{9,15},{10,... | collective-permute-start | bytes 3145736 | tf_op jit(solution)/shard_map/ppermute | solution.py:42
  77.9 22.2 %conditional.7 = (bf16[512,1024]{1,0:T(8,128)(2,1)}) conditional(s32[]{:T(128)} %clamp.4, bf16[512,1024]{1,0:T(8,128)(2,1)} %get-tuple-element.90, bf16[512,1024]{1,0:T(8,128)(2,1)} %get-tuple-element.90, bf16[512,1024]{1,0:T(8,128)(2,1)} %get-tuple-element.90), branch_computations={%region_0.1_spmd, %region_1.2_spmd, %region_2.3_spmd} | conditional | bytes 4194352 | solution.py:57
  77.9 1.3 collective-permute-start
  79.1 20.9 %collective-permute-done = bf16[512,1024]{1,0:T(8,128)(2,1)} collective-permute-done((bf16[512,1024]{1,0:T(8,128)(2,1)}, bf16[512,1024]{1,0:T(8,128)(2,1)}, u32[]{:S(2)}, u32[]{:S(2)}) %collective-permute-start) | collective-permute-done | bytes 1048608 | tf_op jit(solution)/shard_map/cond/branch_0_fun/ppermute | solution.py:55
  100.8 0.9 collective-permute-start.25
  101.9 5.2 %fusion.4 = (bf16[512,1024]{1,0:T(8,128)(2,1)S(1)}, f32[512,1024]{1,0:T(8,128)}) fusion(bf16[512,1024]{1,0:T(8,128)(2,1)} %collective-permute-done.18.refs_4_, bf16[512,1024]{1,0:T(8,128)(2,1)} %collective-permute-done.15.refs_2_, bf16[512,1024]{1,0:T(8,128)(2,1)} %collective-permute-done.17.refs_3_, bf16[512,1024]{1,0:T(8,128)(2,1)} %copy-done.14, ...), kind=kLoop, calls=%fused_computation.18 | loop fusion | flops 5242880 | bytes 9437184 | tf_op jit(solution)/shard_map/convert_element_type | solution.py:449
  107.1 3.0 %unpack.2.refs_1_.refs_8_ = bf16[512,8192]{1,0:T(8,128)(2,1)} custom-call(s32[4]{0:T(128)S(1)} %pad_add_fusion.1.idx_ref, bf16[512,8192]{1,0:T(8,128)(2,1)} %get-tuple-element.94.old_ref, bf16[4,512,512]{2,1,0:T(8,128)(2,1)} %collective-permute-done.23.piece_ref), custom_call_target="tpu_custom_call", output_to_operand_aliasing={{}: (1, {})} | custom-call | bytes 4194304 | tf_op jit(solution)/shard_map/unpack/pallas_call | solution.py:185
  110.1 3.4 %copy-done = bf16[512,8192]{1,0:T(8,128)(2,1)S(1)} copy-done((bf16[512,8192]{1,0:T(8,128)(2,1)S(1)}, bf16[512,8192]{1,0:T(8,128)(2,1)}, u32[]{:S(2)}) %copy-start) | copy-done | bytes 8388632
  113.4 21.3 %conditional.9 = (bf16[512,1024]{1,0:T(8,128)(2,1)}, bf16[512,1024]{1,0:T(8,128)(2,1)S(1)}) conditional(s32[]{:T(128)} %clamp.4, bf16[512,1024]{1,0:T(8,128)(2,1)S(1)} %held_until.10, bf16[512,1024]{1,0:T(8,128)(2,1)S(1)} %held_until.10, bf16[512,1024]{1,0:T(8,128)(2,1)S(1)} %held_until.10), branch_computations={%region_3.4_spmd, %region_4.5_spmd, %region_5.6_spmd} | conditional | bytes 6291512
  113.4 1.2 collective-permute-start.3
  114.6 18.9 %collective-permute-done.3 = bf16[512,1024]{1,0:T(8,128)(2,1)} collective-permute-done((bf16[512,1024]{1,0:T(8,128)(2,1)S(1)}, bf16[512,1024]{1,0:T(8,128)(2,1)}, u32[]{:S(2)}, u32[]{:S(2)}) %collective-permute-start.3) | collective-permute-done | bytes 1048608 | tf_op jit(solution)/shard_map/cond/branch_0_fun/ppermute | solution.py:55
  133.5 1.2 copy.40
  134.8 1.5 slice.48.refs_4_
  136.6 1.1 slice.49.refs_5_
  137.7 2.5 %collective-permute-start.22 = (bf16[256,1024]{1,0:T(8,128)(2,1)S(1)}, bf16[256,1024]{1,0:T(8,128)(2,1)S(1)}, u32[]{:S(2)}, u32[]{:S(2)}) collective-permute-start(bf16[256,1024]{1,0:T(8,128)(2,1)S(1)} %slice.49.refs_5_), channel_id=1, source_target_pairs={{0,6},{1,7},{2,0},{3,1},{4,2},{5,3},{6,4},{7,5},{8,14},{9,15},{10,... | collective-permute-start | bytes 1572872 | tf_op jit(solution)/shard_map/ppermute | solution.py:42
  140.2 1.6 copy-done.11
  141.8 13.7 %forward.3 = (f32[512,1024]{1,0:T(8,128)S(1)}, bf16[512,1024]{1,0:T(8,128)(2,1)}, bf16[512,8192]{1,0:T(8,128)(2,1)}, bf16[3,512,512]{2,1,0:T(8,128)(2,1)}) custom-call(s32[3]{0:T(128)S(1)} %pad_add_fusion.2.idx_ref, bf16[512,8192]{1,0:T(8,128)(2,1)} %bitcast.35, ...), custom_call_target="tpu_custom_call", output_to_operand_aliasing={{2}: (13, {})} | custom-call | flops 6442450944 | bytes 17825792 | tf_op jit(solution)/shard_map/forward/pallas_call | solution.py:322
  155.5 6.2 %collective-permute-start.26 = (bf16[3,512,512]{2,1,0:T(8,128)(2,1)}, bf16[3,512,512]{2,1,0:T(8,128)(2,1)}, u32[]{:S(2)}, u32[]{:S(2)}) collective-permute-start(bf16[3,512,512]{2,1,0:T(8,128)(2,1)} %get-tuple-element.101), channel_id=1, source_target_pairs={{0,1},{1,0},{2,3},{3,2},{4,5},{5,4},{6,7},{7,6},{8,9},{9,8},{10,11... | collective-permute-start | bytes 4718600 | tf_op jit(solution)/shard_map/ppermute | solution.py:50
  161.8 2.3 %fusion = (f32[512,1024]{1,0:T(8,128)S(1)}, f32[512,1024]{1,0:T(8,128)S(1)}) fusion(f32[512,1024]{1,0:T(8,128)S(1)} %copy-done.16, bf16[512,1024]{1,0:T(8,128)(2,1)S(1)} %copy-done.18, bf16[512,1024]{1,0:T(8,128)(2,1)} %get-tuple-element.121.refs_5_, f32[1,512,1024]{2,1,0:T(8,128)S(1)} %copy-done.15), kind=kLoop, calls=%fused_computation.2 | loop fusion | flops 5242880 | bytes 10485760 | tf_op jit(solution)/shard_map/mul | solution.py:454
  164.1 0.7 collective-permute-start.27
  165.4 0.7 copy-done.9
  166.8 3.0 %unpack.3.rest_0_ = bf16[512,8192]{1,0:T(8,128)(2,1)} custom-call(s32[3]{0:T(128)S(1)} %pad_add_fusion.3.idx_ref, bf16[512,8192]{1,0:T(8,128)(2,1)} %get-tuple-element.100.old_ref, bf16[3,512,512]{2,1,0:T(8,128)(2,1)} %collective-permute-done.26.piece_ref), custom_call_target="tpu_custom_call", output_to_operand_aliasing={{}: (1, {})} | custom-call | bytes 3145728 | tf_op jit(solution)/shard_map/unpack/pallas_call | solution.py:185
  169.9 3.4 %copy-done.2 = bf16[1,512,8192]{2,1,0:T(8,128)(2,1)S(1)} copy-done((bf16[1,512,8192]{2,1,0:T(8,128)(2,1)S(1)}, bf16[1,512,8192]{2,1,0:T(8,128)(2,1)}, u32[]{:S(2)}) %copy-start.2) | copy-done | bytes 8388632
  173.3 2.2 %one_shard.2 = (f32[512,1024]{1,0:T(8,128)S(1)}, bf16[512,8192]{1,0:T(8,128)(2,1)}) custom-call(s32[1]{0:T(128)} %bitcast.11.idx_ref, bf16[512,8192]{1,0:T(8,128)(2,1)S(1)} %bitcast.37, bf16[512,1024]{1,0:T(8,128)(2,1)S(1)} %bitcast.46, bf16[512,1024]{1,0:T(8,128)(2,1)S(1)} %held_until.11.w_ref, ...), custom_call_target="tpu_custom_call", output_to_operand_aliasing={{1}: (5, {})} | custom-call | flops 1073741824 | bytes 8388608 | tf_op jit(solution)/shard_map/one_shard/pallas_call | solution.py:384
  175.6 3.6 %one_shard.3 = (bf16[512,1024]{1,0:T(8,128)(2,1)}, bf16[512,8192]{1,0:T(8,128)(2,1)}) custom-call(s32[1]{0:T(128)} %bitcast.idx_ref, bf16[512,8192]{1,0:T(8,128)(2,1)S(1)} %bitcast.40, bf16[512,1024]{1,0:T(8,128)(2,1)S(1)} %bitcast.47, bf16[512,1024]{1,0:T(8,128)(2,1)} %collective-permute-done.24.w_ref, ...), custom_call_target="tpu_custom_call", output_to_operand_aliasing={{1}: (6, {})} | custom-call | flops 1073741824 | bytes 8388608 | tf_op jit(solution)/shard_map/one_shard/pallas_call | solution.py:384
  (76 shorter events, 4.8 us)
Async XLA Ops:
  0.6 24.3 %collective-permute-start.8 = (bf16[512,8192]{1,0:T(8,128)(2,1)}, bf16[512,8192]{1,0:T(8,128)(2,1)}, u32[]{:S(2)}, u32[]{:S(2)}) collective-permute-start(bf16[512,8192]{1,0:T(8,128)(2,1)} %bitcast.31), channel_id=1, source_target_pairs={{0,1},{1,0},{2,3},{3,2},{4,5},{5,4},{6,7},{7,6},{8,9},{9,8},{10,11... | collective-permute-start | bytes 25165832 | tf_op jit(solution)/shard_map/ppermute | solution.py:50
  7.1 10.3 %collective-permute-start.9 = (bf16[512,1536]{1,0:T(8,128)(2,1)}, bf16[512,1536]{1,0:T(8,128)(2,1)S(1)}, u32[]{:S(2)}, u32[]{:S(2)}) collective-permute-start(bf16[512,1536]{1,0:T(8,128)(2,1)} %pack_first.1), channel_id=1, source_target_pairs={{0,1},{1,0},{2,3},{3,2},{4,5},{5,4},{6,7},{7,6},{8,9},{9,8},{10,11... | collective-permute-start | bytes 4718600 | tf_op jit(solution)/shard_map/ppermute | solution.py:50
  7.3 38.4 %collective-permute-start.6 = (bf16[512,1024]{1,0:T(8,128)(2,1)}, bf16[512,1024]{1,0:T(8,128)(2,1)}, u32[]{:S(2)}, u32[]{:S(2)}) collective-permute-start(bf16[512,1024]{1,0:T(8,128)(2,1)} %bitcast_convert_fusion.after_ref.refs_3_.refs_1_), channel_id=1, source_target_pairs={{0,2},{1,3},{2,4},{3,5},{4,6},{5,7},{6,0},{7,1},{8,10},{9,11},{10,... | collective-permute-start | bytes 3145736 | tf_op jit(solution)/shard_map/ppermute | solution.py:38
  8.7 37.0 %collective-permute-start.7 = (bf16[512,1024]{1,0:T(8,128)(2,1)}, bf16[512,1024]{1,0:T(8,128)(2,1)}, u32[]{:S(2)}, u32[]{:S(2)}) collective-permute-start(bf16[512,1024]{1,0:T(8,128)(2,1)} %bitcast_convert_fusion.after_ref.refs_3_.refs_1_), channel_id=1, source_target_pairs={{0,8},{1,9},{2,10},{3,11},{4,12},{5,13},{6,14},{7,15},{8,0},{9,1},... | collective-permute-start | bytes 3145736 | tf_op jit(solution)/shard_map/ppermute | solution.py:46
  10.3 35.4 %collective-permute-start.12 = (bf16[512,1024]{1,0:T(8,128)(2,1)}, bf16[512,1024]{1,0:T(8,128)(2,1)}, u32[]{:S(2)}, u32[]{:S(2)}) collective-permute-start(bf16[512,1024]{1,0:T(8,128)(2,1)} %bitcast_convert_fusion.after_ref.refs_3_.refs_1_), channel_id=1, source_target_pairs={{0,6},{1,7},{2,0},{3,1},{4,2},{5,3},{6,4},{7,5},{8,14},{9,15},{10,... | collective-permute-start | bytes 3145736 | tf_op jit(solution)/shard_map/ppermute | solution.py:42
  17.4 1.1 copy-start.4
  23.5 21.1 %collective-permute-start.10 = (bf16[256,1024]{1,0:T(8,128)(2,1)}, bf16[256,1024]{1,0:T(8,128)(2,1)S(1)}, u32[]{:S(2)}, u32[]{:S(2)}) collective-permute-start(bf16[256,1024]{1,0:T(8,128)(2,1)} %get-tuple-element.79), channel_id=1, source_target_pairs={{0,2},{1,3},{2,4},{3,5},{4,6},{5,7},{6,0},{7,1},{8,10},{9,11},{10,... | collective-permute-start | bytes 1572872 | tf_op jit(solution)/shard_map/ppermute | solution.py:38
  24.9 1.6 copy-start.3
  24.9 1.7 copy-start.5
  24.9 20.5 %collective-permute-start.11 = (bf16[256,1024]{1,0:T(8,128)(2,1)}, bf16[256,1024]{1,0:T(8,128)(2,1)S(1)}, u32[]{:S(2)}, u32[]{:S(2)}) collective-permute-start(bf16[256,1024]{1,0:T(8,128)(2,1)} %held_until.6), channel_id=1, source_target_pairs={{0,6},{1,7},{2,0},{3,1},{4,2},{5,3},{6,4},{7,5},{8,14},{9,15},{10,... | collective-permute-start | bytes 1572872 | tf_op jit(solution)/shard_map/ppermute | solution.py:42
  26.7 3.4 %copy-start.1 = (bf16[1,512,8192]{2,1,0:T(8,128)(2,1)S(1)}, bf16[1,512,8192]{2,1,0:T(8,128)(2,1)}, u32[]{:S(2)}) copy-start(bf16[1,512,8192]{2,1,0:T(8,128)(2,1)} %param.16) | copy-start | bytes 25165828
  44.1 1.7 copy-start.14
  45.7 24.4 %collective-permute-start.16 = (bf16[512,1024]{1,0:T(8,128)(2,1)S(1)}, bf16[512,1024]{1,0:T(8,128)(2,1)S(1)}, u32[]{:S(2)}, u32[]{:S(2)}) collective-permute-start(bf16[512,1024]{1,0:T(8,128)(2,1)S(1)} %get-tuple-element.86.refs_4_), channel_id=1, source_target_pairs={{0,2},{1,3},{2,4},{3,5},{4,6},{5,7},{6,0},{7,1},{8,10},{9,11},{10,... | collective-permute-start | bytes 3145736 | tf_op jit(solution)/shard_map/ppermute | solution.py:38
  47.2 24.3 %collective-permute-start.13 = (bf16[512,1024]{1,0:T(8,128)(2,1)S(1)}, bf16[512,1024]{1,0:T(8,128)(2,1)S(1)}, u32[]{:S(2)}, u32[]{:S(2)}) collective-permute-start(bf16[512,1024]{1,0:T(8,128)(2,1)S(1)} %get-tuple-element.83.refs_5_), channel_id=1, source_target_pairs={{0,8},{1,9},{2,10},{3,11},{4,12},{5,13},{6,14},{7,15},{8,0},{9,1},... | collective-permute-start | bytes 3145736 | tf_op jit(solution)/shard_map/ppermute | solution.py:46
  48.1 23.4 %collective-permute-start.14 = (bf16[512,1024]{1,0:T(8,128)(2,1)S(1)}, bf16[512,1024]{1,0:T(8,128)(2,1)S(1)}, u32[]{:S(2)}, u32[]{:S(2)}) collective-permute-start(bf16[512,1024]{1,0:T(8,128)(2,1)S(1)} %get-tuple-element.84.refs_6_), channel_id=1, source_target_pairs={{0,6},{1,7},{2,0},{3,1},{4,2},{5,3},{6,4},{7,5},{8,14},{9,15},{10,... | collective-permute-start | bytes 3145736 | tf_op jit(solution)/shard_map/ppermute | solution.py:42
  64.6 8.5 %copy-start.10 = (f32[512,1024]{1,0:T(8,128)}, f32[512,1024]{1,0:T(8,128)S(1)}, u32[]{:S(2)}) copy-start(f32[512,1024]{1,0:T(8,128)S(1)} %get-tuple-element.98.refs_7_) | copy-start | bytes 6291460
  64.7 8.5 %copy-start.6 = (f32[512,1024]{1,0:T(8,128)}, f32[512,1024]{1,0:T(8,128)S(1)}, u32[]{:S(2)}) copy-start(f32[512,1024]{1,0:T(8,128)S(1)} %get-tuple-element.87.refs_2_.refs_6_) | copy-start | bytes 6291460
  64.7 42.4 %collective-permute-start.23 = (bf16[4,512,512]{2,1,0:T(8,128)(2,1)}, bf16[4,512,512]{2,1,0:T(8,128)(2,1)}, u32[]{:S(2)}, u32[]{:S(2)}) collective-permute-start(bf16[4,512,512]{2,1,0:T(8,128)(2,1)} %get-tuple-element.95), channel_id=1, source_target_pairs={{0,1},{1,0},{2,3},{3,2},{4,5},{5,4},{6,7},{7,6},{8,9},{9,8},{10,11... | collective-permute-start | bytes 6291464 | tf_op jit(solution)/shard_map/ppermute | solution.py:50
  73.2 26.9 %collective-permute-start.17 = (bf16[512,1024]{1,0:T(8,128)(2,1)}, bf16[512,1024]{1,0:T(8,128)(2,1)}, u32[]{:S(2)}, u32[]{:S(2)}) collective-permute-start(bf16[512,1024]{1,0:T(8,128)(2,1)} %get-tuple-element.89), channel_id=1, source_target_pairs={{0,2},{1,3},{2,4},{3,5},{4,6},{5,7},{6,0},{7,1},{8,10},{9,11},{10,... | collective-permute-start | bytes 3145736 | tf_op jit(solution)/shard_map/ppermute | solution.py:38
  73.9 26.1 %collective-permute-start.18 = (bf16[512,1024]{1,0:T(8,128)(2,1)}, bf16[512,1024]{1,0:T(8,128)(2,1)}, u32[]{:S(2)}, u32[]{:S(2)}) collective-permute-start(bf16[512,1024]{1,0:T(8,128)(2,1)} %add_convert_fusion.refs_4_), channel_id=1, source_target_pairs={{0,8},{1,9},{2,10},{3,11},{4,12},{5,13},{6,14},{7,15},{8,0},{9,1},... | collective-permute-start | bytes 3145736 | tf_op jit(solution)/shard_map/ppermute | solution.py:46
  74.8 25.2 %collective-permute-start.15 = (bf16[512,1024]{1,0:T(8,128)(2,1)}, bf16[512,1024]{1,0:T(8,128)(2,1)}, u32[]{:S(2)}, u32[]{:S(2)}) collective-permute-start(bf16[512,1024]{1,0:T(8,128)(2,1)} %add_convert_fusion.1.refs_3_), channel_id=1, source_target_pairs={{0,6},{1,7},{2,0},{3,1},{4,2},{5,3},{6,4},{7,5},{8,14},{9,15},{10,... | collective-permute-start | bytes 3145736 | tf_op jit(solution)/shard_map/ppermute | solution.py:42
  77.9 22.2 %collective-permute-start = (bf16[512,1024]{1,0:T(8,128)(2,1)}, bf16[512,1024]{1,0:T(8,128)(2,1)}, u32[]{:S(2)}, u32[]{:S(2)}) collective-permute-start(bf16[512,1024]{1,0:T(8,128)(2,1)} %param.4), channel_id=1, source_target_pairs={{0,16},{16,0},{32,48},{48,32},{64,80},{80,64},{96,112},{112,96},{1... | collective-permute-start | bytes 3145736 | tf_op jit(solution)/shard_map/cond/branch_0_fun/ppermute | solution.py:55
  100.1 34.7 %collective-permute-start.19 = (bf16[512,1024]{1,0:T(8,128)(2,1)}, bf16[512,1024]{1,0:T(8,128)(2,1)}, u32[]{:S(2)}, u32[]{:S(2)}) collective-permute-start(bf16[512,1024]{1,0:T(8,128)(2,1)} %get-tuple-element.91), channel_id=1, source_target_pairs={{0,8},{1,9},{2,10},{3,11},{4,12},{5,13},{6,14},{7,15},{8,0},{9,1},... | collective-permute-start | bytes 3145736 | tf_op jit(solution)/shard_map/ppermute | solution.py:46
  100.2 36.5 %collective-permute-start.21 = (bf16[512,1024]{1,0:T(8,128)(2,1)}, bf16[512,1024]{1,0:T(8,128)(2,1)}, u32[]{:S(2)}, u32[]{:S(2)}) collective-permute-start(bf16[512,1024]{1,0:T(8,128)(2,1)} %get-tuple-element.92), channel_id=1, source_target_pairs={{0,6},{1,7},{2,0},{3,1},{4,2},{5,3},{6,4},{7,5},{8,14},{9,15},{10,... | collective-permute-start | bytes 3145736 | tf_op jit(solution)/shard_map/ppermute | solution.py:42
  100.8 39.4 %collective-permute-start.25 = (bf16[512,1024]{1,0:T(8,128)(2,1)}, bf16[512,1024]{1,0:T(8,128)(2,1)}, u32[]{:S(2)}, u32[]{:S(2)}) collective-permute-start(bf16[512,1024]{1,0:T(8,128)(2,1)} %get-tuple-element.91), channel_id=1, source_target_pairs={{0,2},{1,3},{2,4},{3,5},{4,6},{5,7},{6,0},{7,1},{8,10},{9,11},{10,... | collective-permute-start | bytes 3145736 | tf_op jit(solution)/shard_map/ppermute | solution.py:38
  110.0 3.4 %copy-start = (bf16[512,8192]{1,0:T(8,128)(2,1)S(1)}, bf16[512,8192]{1,0:T(8,128)(2,1)}, u32[]{:S(2)}) copy-start(bf16[512,8192]{1,0:T(8,128)(2,1)} %unpack.2.refs_1_.refs_8_) | copy-start | bytes 25165828
  113.4 20.1 %collective-permute-start.3 = (bf16[512,1024]{1,0:T(8,128)(2,1)S(1)}, bf16[512,1024]{1,0:T(8,128)(2,1)}, u32[]{:S(2)}, u32[]{:S(2)}) collective-permute-start(bf16[512,1024]{1,0:T(8,128)(2,1)S(1)} %param.7), channel_id=1, source_target_pairs={{0,16},{16,0},{32,48},{48,32},{64,80},{80,64},{96,112},{112,96},{1... | collective-permute-start | bytes 3145736 | tf_op jit(solution)/shard_map/cond/branch_0_fun/ppermute | solution.py:55
  134.8 5.4 %copy-start.17 = (bf16[512,1024]{1,0:T(8,128)(2,1)}, bf16[512,1024]{1,0:T(8,128)(2,1)S(1)}, u32[]{:S(2)}) copy-start(bf16[512,1024]{1,0:T(8,128)(2,1)S(1)} %get-tuple-element.110) | copy-start | bytes 3145732
  134.8 5.4 %copy-start.7 = (f32[512,1024]{1,0:T(8,128)S(1)}, f32[512,1024]{1,0:T(8,128)}, u32[]{:S(2)}) copy-start(f32[512,1024]{1,0:T(8,128)} %copy-done.6) | copy-start | bytes 6291460
  136.3 28.6 %collective-permute-start.20 = (bf16[256,1024]{1,0:T(8,128)(2,1)S(1)}, bf16[256,1024]{1,0:T(8,128)(2,1)S(1)}, u32[]{:S(2)}, u32[]{:S(2)}) collective-permute-start(bf16[256,1024]{1,0:T(8,128)(2,1)S(1)} %slice.48.refs_4_), channel_id=1, source_target_pairs={{0,2},{1,3},{2,4},{3,5},{4,6},{5,7},{6,0},{7,1},{8,10},{9,11},{10,... | collective-permute-start | bytes 1572872 | tf_op jit(solution)/shard_map/ppermute | solution.py:38
  137.7 27.1 %collective-permute-start.22 = (bf16[256,1024]{1,0:T(8,128)(2,1)S(1)}, bf16[256,1024]{1,0:T(8,128)(2,1)S(1)}, u32[]{:S(2)}, u32[]{:S(2)}) collective-permute-start(bf16[256,1024]{1,0:T(8,128)(2,1)S(1)} %slice.49.refs_5_), channel_id=1, source_target_pairs={{0,6},{1,7},{2,0},{3,1},{4,2},{5,3},{6,4},{7,5},{8,14},{9,15},{10,... | collective-permute-start | bytes 1572872 | tf_op jit(solution)/shard_map/ppermute | solution.py:42
  140.2 1.6 copy-start.11
  141.8 20.0 %copy-start.15 = (f32[1,512,1024]{2,1,0:T(8,128)S(1)}, f32[1,512,1024]{2,1,0:T(8,128)}, u32[]{:S(2)}) copy-start(f32[1,512,1024]{2,1,0:T(8,128)} %param.18) | copy-start | bytes 6291460
  141.8 20.0 %copy-start.16 = (f32[512,1024]{1,0:T(8,128)S(1)}, f32[512,1024]{1,0:T(8,128)}, u32[]{:S(2)}) copy-start(f32[512,1024]{1,0:T(8,128)} %get-tuple-element.112) | copy-start | bytes 6291460
  141.8 20.0 %copy-start.18 = (bf16[512,1024]{1,0:T(8,128)(2,1)S(1)}, bf16[512,1024]{1,0:T(8,128)(2,1)}, u32[]{:S(2)}) copy-start(bf16[512,1024]{1,0:T(8,128)(2,1)} %copy-done.17) | copy-start | bytes 3145732
  155.5 8.6 %copy-start.12 = (f32[512,1024]{1,0:T(8,128)}, f32[512,1024]{1,0:T(8,128)S(1)}, u32[]{:S(2)}) copy-start(f32[512,1024]{1,0:T(8,128)S(1)} %get-tuple-element.99.key_ref) | copy-start | bytes 6291460
  155.5 11.3 %collective-permute-start.26 = (bf16[3,512,512]{2,1,0:T(8,128)(2,1)}, bf16[3,512,512]{2,1,0:T(8,128)(2,1)}, u32[]{:S(2)}, u32[]{:S(2)}) collective-permute-start(bf16[3,512,512]{2,1,0:T(8,128)(2,1)} %get-tuple-element.101), channel_id=1, source_target_pairs={{0,1},{1,0},{2,3},{3,2},{4,5},{5,4},{6,7},{7,6},{8,9},{9,8},{10,11... | collective-permute-start | bytes 4718600 | tf_op jit(solution)/shard_map/ppermute | solution.py:50
  164.1 1.3 copy-start.8
  164.1 2.0 %copy-start.9 = (f32[512,1024]{1,0:T(8,128)}, f32[512,1024]{1,0:T(8,128)S(1)}, u32[]{:S(2)}) copy-start(f32[512,1024]{1,0:T(8,128)S(1)} %get-tuple-element.114.refs_1_) | copy-start | bytes 6291460
  164.1 11.4 %collective-permute-start.27 = (bf16[512,1024]{1,0:T(8,128)(2,1)}, bf16[512,1024]{1,0:T(8,128)(2,1)S(1)}, u32[]{:S(2)}, u32[]{:S(2)}) collective-permute-start(bf16[512,1024]{1,0:T(8,128)(2,1)} %get-tuple-element.103), channel_id=1, source_target_pairs={{0,1},{1,0},{2,3},{3,2},{4,5},{5,4},{6,7},{7,6},{8,9},{9,8},{10,11... | collective-permute-start | bytes 3145736 | tf_op jit(solution)/shard_map/ppermute | solution.py:50
  166.1 9.4 %collective-permute-start.24 = (bf16[512,1024]{1,0:T(8,128)(2,1)S(1)}, bf16[512,1024]{1,0:T(8,128)(2,1)}, u32[]{:S(2)}, u32[]{:S(2)}) collective-permute-start(bf16[512,1024]{1,0:T(8,128)(2,1)S(1)} %held_until.11.w_ref), channel_id=1, source_target_pairs={{0,1},{1,0},{2,3},{3,2},{4,5},{5,4},{6,7},{7,6},{8,9},{9,8},{10,11... | collective-permute-start | bytes 3145736 | tf_op jit(solution)/shard_map/ppermute | solution.py:50
  166.8 3.1 %copy-start.13 = (f32[512,1024]{1,0:T(8,128)S(1)}, f32[512,1024]{1,0:T(8,128)}, u32[]{:S(2)}) copy-start(f32[512,1024]{1,0:T(8,128)} %copy-done.12) | copy-start | bytes 6291460
  166.8 8.7 %slice-start = ((s8[8388608]{0:T(1024)(128)(4,1)}), s8[4194304]{0:T(1024)(128)(4,1)S(1)}, s32[]{:S(2)}) async-start(s8[8388608]{0:T(1024)(128)(4,1)} %bitcast.38), calls=%async_computation | async-start | bytes 8388608
  169.9 3.4 %copy-start.2 = (bf16[1,512,8192]{2,1,0:T(8,128)(2,1)S(1)}, bf16[1,512,8192]{2,1,0:T(8,128)(2,1)}, u32[]{:S(2)}) copy-start(bf16[1,512,8192]{2,1,0:T(8,128)(2,1)} %param.16) | copy-start | bytes 25165828
  173.3 2.3 %slice-start.1 = ((s8[8388608]{0:T(1024)(128)(4,1)}), s8[4194304]{0:T(1024)(128)(4,1)S(1)}, s32[]{:S(2)}) async-start(s8[8388608]{0:T(1024)(128)(4,1)} %bitcast.38), calls=%async_computation.1 | async-start | bytes 8388608
